TPU v7x, 32 devices: a whole 2x2x4 slice. The times are simulated.
32 devices in a mesh: fsdp: 4 (over y, core), ctx: 8 (over z, x).
Axes of the slice: x: 2, y: 2, z: 4, core: 2. Of those that a mesh axis runs over, the one named last changes fastest.
Arguments:
- tokens: bfloat16 [1024, 8, 1152], P('ctx', 'fsdp'), may hold values from -6 to 6
- w_query: bfloat16 [1152, 1152], P('fsdp'), may hold values from -0.1875 to 0.1875
- w_key: bfloat16 [1152, 384], P('fsdp'), may hold values from -0.1875 to 0.1875
- w_value: bfloat16 [1152, 384], P('fsdp'), may hold values from -0.1875 to 0.1875
- w_out: bfloat16 [1152, 1152], P('fsdp'), may hold values from -1.5 to 1.5
- w_gate: bfloat16 [1152, 3072], P('fsdp'), may hold values from -0.1875 to 0.1875
- w_up: bfloat16 [1152, 3072], P('fsdp'), may hold values from -0.1875 to 0.1875
- w_down: bfloat16 [3072, 1152], P('fsdp'), may hold values from -0.109375 to 0.109375
- gain_attn: bfloat16 [1152], P('fsdp'), may hold values from 0.5 to 1.5
- gain_ffn: bfloat16 [1152], P('fsdp'), may hold values from 0.5 to 1.5
- cotangent: bfloat16 [1024, 8, 1152], P('ctx', 'fsdp'), may hold values from -6 to 6
Outputs:
- layer_out: bfloat16 [1024, 8, 1152], P('ctx', 'fsdp')
- grad_tokens: float32 [1024, 8, 1152], P('ctx', 'fsdp')
- grad_query: float32 [1152, 1152], P('fsdp')
- grad_key: float32 [1152, 384], P('fsdp')
- grad_value: float32 [1152, 384], P('fsdp')
- grad_out: float32 [1152, 1152], P('fsdp')
- grad_gate: float32 [1152, 3072], P('fsdp')
- grad_up: float32 [1152, 3072], P('fsdp')
- grad_down: float32 [3072, 1152], P('fsdp')
- grad_gain_attn: float32 [1152], P('fsdp')
- grad_gain_ffn: float32 [1152], P('fsdp')
All inputs are finite; a program needn't handle non-finite values.
Results may differ from a plain program's by a relative error of at most 0.023.
Values may be sent and summed in bfloat16 or wider, within the bound.
A program may use at most 320 MiB of HBM per device.

v0:
```python
import functools

import jax
import jax.numpy as jnp
from jax import lax
from jax.experimental import pallas as pl
from jax.experimental.pallas import tpu as pltpu
from jax.sharding import PartitionSpec as P

H = 18
KVH = 6
HD = 64
FF = 3072


EPSILON = 1e-05
ROTARY_BASE = 10000.0
MASKED_SCORE = -1e30


def norm_scale(rows):
    return lax.rsqrt(jnp.mean(rows * rows, axis=-1, keepdims=True) + EPSILON)


def forward_dot(left, right):
    return jnp.dot(left, right, preferred_element_type=jnp.float32)


MESH = pl.DeviceIdType.MESH
LANES = 128


def ring_place(ctx, fsdp, count):
    column, side = lax.div(ctx, 2), lax.rem(ctx, 2)
    place = column + side * (count - 1 - 2 * column)
    odd = lax.rem(fsdp, 2)
    return place + odd * (count - 1 - 2 * place)


def ring_ctx(place, fsdp, count):
    odd = lax.rem(fsdp, 2)
    place = place + odd * (count - 1 - 2 * place)
    late = lax.div(place, count // 2)
    return (1 - late) * 2 * place + late * (2 * (count - 1 - place) + 1)


class GroupGather:
    def __init__(self, shard_of, sends, arrivals):
        self.shard_of, self.sends, self.arrivals = shard_of, sends, arrivals
        self.fsdp, self.ctx = lax.axis_index("fsdp"), lax.axis_index("ctx")
        self.chips = lax.axis_size("fsdp") // 2
        self.chip, self.core = lax.div(self.fsdp, 2), lax.rem(self.fsdp, 2)
        self.sibling = 2 * self.chip + 1 - self.core

    def copy(self, source, shard, semaphore, device):
        return pltpu.make_async_remote_copy(
            src_ref=source,
            dst_ref=self.shard_of(shard),
            send_sem=self.sends.at[semaphore],
            recv_sem=self.arrivals.at[semaphore],
            device_id=(device, self.ctx),
            device_id_type=MESH,
        )

    def same_core(self, step):
        return 2 * lax.rem(self.chip + step, self.chips) + self.core

    def across(self, source):
        return self.copy(source, self.fsdp, 0, self.sibling)

    def out(self, source, step):
        return self.copy(source, self.fsdp, step, self.same_core(step))

    def onward(self, step):
        shard = self.same_core(self.chips - step)
        return self.copy(self.shard_of(shard), shard, self.chips - 1 + step, self.sibling)

    def start(self, source):
        for step in range(1, self.chips):
            self.out(source, step).start()
        self.across(source).start()

    def forward(self):
        own = self.shard_of(self.fsdp)
        for step in range(1, self.chips):
            self.out(own, step).wait_recv()
            self.onward(step).start()

    def sibling_here(self):
        self.across(self.shard_of(self.fsdp)).wait_recv()

    def crossed(self, step):
        self.onward(step).wait_recv()

    def sent(self):
        own = self.shard_of(self.fsdp)
        self.across(own).wait_send()
        for step in range(1, self.chips):
            self.out(own, step).wait_send()
            self.onward(step).wait_send()

    def finish(self):
        self.forward()
        self.sibling_here()
        for step in range(1, self.chips):
            self.crossed(step)
        self.sent()


class HalfGather:
    def __init__(self, held, own_rows, sends, arrivals):
        self.held, self.own = held, own_rows
        self.sends, self.arrivals = sends, arrivals
        self.fsdp, self.ctx = lax.axis_index("fsdp"), lax.axis_index("ctx")
        self.chips = lax.axis_size("fsdp") // 2
        self.chip, self.core = lax.div(self.fsdp, 2), lax.rem(self.fsdp, 2)
        self.sibling = 2 * self.chip + 1 - self.core
        self.side = lax.rem(self.ctx, 2)
        self.pair = self.ctx + 1 - 2 * self.side
        first = -(-own_rows // 32) * 16
        self.halves = ((0, first), (first, own_rows - first))

    def same_core(self, step):
        return 2 * lax.rem(self.chip + step, self.chips) + self.core

    def rows(self, shard, half=None):
        begin, size = (0, self.own) if half is None else self.halves[half]
        return self.held.at[pl.ds(shard * self.own + begin, size)]

    def copy(self, source, target, semaphore, device):
        return pltpu.make_async_remote_copy(
            src_ref=source,
            dst_ref=target,
            send_sem=self.sends.at[semaphore],
            recv_sem=self.arrivals.at[semaphore],
            device_id=device,
            device_id_type=MESH,
        )

    def on_side(self, body):
        for half in range(2):

            @pl.when(self.side == half)
            def _(half=half):
                body(half)

    def across(self, source):
        return self.copy(source, self.rows(self.fsdp), 0, (self.sibling, self.ctx))

    def out(self, source, step, half):
        begin, size = self.halves[half]
        return self.copy(
            source.at[pl.ds(begin, size)],
            self.rows(self.fsdp, half),
            step,
            (self.same_core(step), self.ctx),
        )

    def to_pair(self, step, half):
        part = self.rows(self.same_core(self.chips - step), half)
        return self.copy(part, part, self.chips - 1 + step, (self.fsdp, self.pair))

    def onward(self, step):
        part = self.rows(self.same_core(self.chips - step))
        return self.copy(part, part, 2 * self.chips - 2 + step, (self.sibling, self.ctx))

    def start(self, source):
        def send(half):
            for step in range(1, self.chips):
                self.out(source, step, half).start()

        self.on_side(send)
        self.across(source).start()

    def to_pairs(self):
        def forward(half):
            for step in range(1, self.chips):
                self.out(self.rows(self.fsdp), step, half).wait_recv()
                self.to_pair(step, half).start()

        self.on_side(forward)

    def to_sibling(self):
        def forward(half):
            for step in range(1, self.chips):
                self.to_pair(step, 1 - half).wait_recv()

        self.on_side(forward)
        for step in range(1, self.chips):
            self.onward(step).start()

    def arrived(self):
        self.across(self.rows(self.fsdp)).wait_recv()
        for step in range(1, self.chips):
            self.onward(step).wait_recv()

    def sent(self):
        def wait(half):
            for step in range(1, self.chips):
                self.out(self.rows(self.fsdp), step, half).wait_send()
                self.to_pair(step, half).wait_send()

        self.on_side(wait)
        self.across(self.rows(self.fsdp)).wait_send()
        for step in range(1, self.chips):
            self.onward(step).wait_send()


def half_semaphores(many):
    return pltpu.SemaphoreType.DMA((many, 3 * (lax.axis_size("fsdp") // 2) - 2))


def group_semaphores():
    return pltpu.SemaphoreType.DMA((lax.axis_size("fsdp") - 1,))


def greet_group(barrier):
    fsdp, ctx, group = lax.axis_index("fsdp"), lax.axis_index("ctx"), lax.axis_size("fsdp")
    for step in range(1, group):
        peer = lax.rem(fsdp + step, group)
        pl.semaphore_signal(barrier, inc=1, device_id=(peer, ctx), device_id_type=MESH)
    return group - 1


class Steps:
    def __init__(self):
        self.fsdp, self.ctx = lax.axis_index("fsdp"), lax.axis_index("ctx")
        self.levels = lax.axis_size("ctx") // 2
        self.level, self.side = lax.div(self.ctx, 2), lax.rem(self.ctx, 2)
        self.peer = (self.fsdp, 2 * self.level + 1 - self.side)
        self.above = (self.fsdp, lax.rem(self.ctx + 2, 2 * self.levels))
        self.below = (self.fsdp, lax.rem(self.ctx + 2 * self.levels - 2, 2 * self.levels))
        self.has_above = self.level + 1 < self.levels
        self.has_below = self.level > 0

    def greet(self, barrier):
        pl.semaphore_signal(barrier, inc=1, device_id=self.peer, device_id_type=MESH)

        @pl.when(self.has_above)
        def _():
            pl.semaphore_signal(barrier, inc=1, device_id=self.above, device_id_type=MESH)

        @pl.when(self.has_below)
        def _():
            pl.semaphore_signal(barrier, inc=1, device_id=self.below, device_id_type=MESH)

        return 1 + jnp.minimum(self.level, 1) + jnp.minimum(self.levels - 1 - self.level, 1)


PARTS = 2


def causal(keys, wide, shape):
    key_at = lax.broadcasted_iota(jnp.int32, shape, 0)
    query_at = lax.rem(lax.broadcasted_iota(jnp.int32, shape, 1), keys)
    return key_at <= query_at


def attend_kernel(
    x_ref, gain_ref, cos_ref, sin_ref, query_ref, key_ref, value_ref, out_ref, gate_ref, up_ref, g_ref,
    q_ref, normed_t_ref, gains_ref, full_query, full_key, full_value,
    low_ref, low_t_ref, mix_ref, log_ref, all_ref, full_out_ref, my_gate_ref, my_up_ref, all_g_ref,
    normed_ref, key_rows, gain_all, own_out, own_gate, own_up, own_g,
    top_ref, total_ref, chain_sends, chain_arrivals, peer_sends, peer_arrivals,
    half_sends, half_arrivals, gain_sends, gain_arrivals,
    out_sends, out_arrivals, g_sends, g_arrivals,
    part_sends, part_arrivals, local_sems,
):
    steps = Steps()
    fsdp, ctx, group = steps.fsdp, steps.ctx, lax.axis_size("fsdp")
    units, deep, wide = q_ref.shape
    keys = all_ref.shape[2]
    per_part = units // PARTS
    rows_count, width = x_ref.shape
    own = query_ref.shape[0]
    sequences, groups = units // KVH, H // KVH
    barrier = pltpu.get_barrier_semaphore()
    greeted = steps.greet(barrier) + greet_group(barrier)
    span = KVH * HD
    pieces = [(key_ref, full_key, 0), (value_ref, full_value, 0)]
    pieces += [(query_ref, full_query, start) for start in range(0, width, span)]
    gathers = []
    for at, (source, target, start) in enumerate(pieces):
        columns = pl.ds(start, span)
        gather = HalfGather(
            target.at[:, columns], own, half_sends.at[at], half_arrivals.at[at]
        )
        gathers.append((gather, source.at[:, columns]))
    own_rows = pl.ds(fsdp * own, own)
    own_copies = [
        pltpu.make_async_copy(source, target.at[own_rows], local_sems.at[4 + at])
        for at, (source, target) in enumerate(
            ((key_ref, full_key), (value_ref, full_value), (query_ref, full_query))
        )
    ]
    for copy in own_copies:
        copy.start()
    gain_all[fsdp] = gain_ref[...]
    pl.semaphore_wait(barrier, greeted)

    def gain_copy(step):
        peer = lax.rem(fsdp + step, group)
        return pltpu.make_async_remote_copy(
            src_ref=gain_ref,
            dst_ref=gain_all.at[fsdp],
            send_sem=gain_sends.at[step - 1],
            recv_sem=gain_arrivals.at[step - 1],
            device_id=(peer, ctx),
            device_id_type=MESH,
        )

    for step in range(1, group):
        gain_copy(step).start()
    for gather, source in gathers:
        gather.start(source)
    inputs = x_ref[...].astype(jnp.float32)
    scale = norm_scale(inputs)
    q_ref[:, HD:, :] = jnp.zeros((units, HD, wide), q_ref.dtype)
    for step in range(1, group):
        gain_copy(step).wait_recv()
    gains = jnp.concatenate([gain_all[shard][:, :own] for shard in range(group)], axis=1)
    gains_ref[...] = gains
    normed_ref[...] = (inputs * scale * gains[:1]).astype(jnp.bfloat16)
    cosine, sine = cos_ref[...], sin_ref[...]

    def turn(columns):
        first, second = columns[: HD // 2], columns[HD // 2 :]
        return jnp.concatenate(
            [first * cosine - second * sine, second * cosine + first * sine], axis=0
        ).astype(jnp.bfloat16)

    def block_copy(level, part, side, semaphores, arrivals, arrives, device):
        block = 2 * (steps.level - level) + side
        held = all_ref.at[block, pl.ds(part * per_part, per_part)]
        return pltpu.make_async_remote_copy(
            src_ref=held,
            dst_ref=held,
            send_sem=semaphores.at[level, part],
            recv_sem=arrivals.at[arrives, part],
            device_id=device,
            device_id_type=MESH,
        )

    def chain(level, part):
        return block_copy(
            level, part, steps.side, chain_sends, chain_arrivals, level + 1, steps.above
        )

    def across(level, part):
        return block_copy(
            level, part, steps.side, peer_sends, peer_arrivals, level, steps.peer
        )

    def pass_on(level, part):
        @pl.when(steps.has_above)
        def _():
            chain(level, part).start()

    def project(at):
        _, weight, start = pieces[at]
        made = forward_dot(normed_ref[...], weight[:, start : start + span])
        if at == 0:
            key_rows[...] = made
            return
        for sequence in range(sequences):
            block = slice(sequence * keys, (sequence + 1) * keys)
            for pair in range(span // (2 * HD)):
                columns = slice(pair * 2 * HD, (pair + 1) * 2 * HD)
                turned = made[block, columns].T
                if at == 1:
                    turned_keys = key_rows[block, columns].T
                    for half in range(2):
                        held = slice(half * HD, (half + 1) * HD)
                        both = jnp.concatenate(
                            [turn(turned_keys[held]), turned[held].astype(jnp.bfloat16)], axis=0
                        )
                        all_ref[ctx, sequence * KVH + 2 * pair + half] = both.T
                else:
                    for half in range(2):
                        head = start // HD + 2 * pair + half
                        unit, member = sequence * KVH + head // groups, head % groups
                        part = turn(turned[half * HD : (half + 1) * HD])
                        q_ref[unit, :HD, member * keys : (member + 1) * keys] = part * jnp.bfloat16(
                            HD ** (-0.5)
                        )
        if at == 1:
            for part in range(PARTS):
                pass_on(0, part)

                @pl.when(steps.side == 0)
                def _():
                    across(0, part).start()

    columns = my_gate_ref.shape[1]
    gathered = HalfGather(full_out_ref, own, out_sends.at[0], out_arrivals.at[0])
    gathered_g = GroupGather(lambda shard: all_g_ref.at[shard], g_sends, g_arrivals)
    mine = lane_tile(fsdp, columns)
    own_parts = (
        (out_ref, own_out, full_out_ref.at[own_rows]),
        (gate_ref.at[:, mine], own_gate, my_gate_ref.at[own_rows]),
        (up_ref.at[:, mine], own_up, my_up_ref.at[own_rows]),
        (g_ref, own_g, all_g_ref.at[fsdp]),
    )
    loads = [
        pltpu.make_async_copy(source, held, local_sems.at[at])
        for at, (source, held, _) in enumerate(own_parts)
    ]
    background = [
        pltpu.make_async_copy(held, target, local_sems.at[at])
        for at, (_, held, target) in enumerate(own_parts)
    ]
    slices = []
    for which, (source, target) in enumerate(((gate_ref, my_gate_ref), (up_ref, my_up_ref))):
        for step in range(1, group):
            peer = lax.rem(fsdp + step, group)
            slices.append(
                pltpu.make_async_remote_copy(
                    src_ref=source.at[:, lane_tile(peer, columns)],
                    dst_ref=target.at[own_rows],
                    send_sem=part_sends.at[which, step - 1],
                    recv_sem=part_arrivals.at[which, step - 1],
                    device_id=(peer, ctx),
                    device_id_type=MESH,
                )
            )

    def start_background():
        for copy in loads:
            copy.start()
        gathered.start(out_ref)
        for copy in slices:
            copy.start()
        gathered_g.start(g_ref)

    last = len(pieces)
    for at in range(last + 2):
        if at < last:
            gathers[at][0].to_pairs()
        if at == last - 1:
            start_background()
        if 1 <= at <= last:
            gathers[at - 1][0].to_sibling()
        if at == 1:
            for column in range(width // LANES):
                columns = slice(column * LANES, (column + 1) * LANES)
                normed_t_ref[columns, :] = normed_ref[:, columns].T
            for copy in own_copies:
                copy.wait()
        if at >= 2:
            gathers[at - 2][0].arrived()
            project(at - 2)

    def second_half():
        gathered.to_pairs()
        for load, copy in zip(loads, background):
            load.wait()
            copy.start()

    def add(unit, kv):
        scores = jnp.dot(kv, q_ref[unit], preferred_element_type=jnp.float32)
        top = top_ref[unit]
        new_top = jnp.maximum(top, jnp.max(scores, axis=0, keepdims=True))
        fade = jnp.exp(top - new_top)
        weights = jnp.exp(scores - new_top)
        top_ref[unit] = new_top
        total_ref[unit] = total_ref[unit] * fade + jnp.sum(weights, axis=0, keepdims=True)
        added = jnp.dot(kv.T, weights.astype(jnp.bfloat16), preferred_element_type=jnp.float32)
        mix_ref[unit] = mix_ref[unit] * fade + added[HD:]

    def over_units(body, first, count):
        def two(at, unused):
            body(first + 2 * at)
            body(first + 2 * at + 1)
            return unused

        lax.fori_loop(0, count // 2, two, 0)

    def diagonal(unit):
        kv = all_ref[ctx, unit]
        scores = jnp.dot(kv, q_ref[unit], preferred_element_type=jnp.float32)
        scores = jnp.where(causal(keys, wide, scores.shape), scores, MASKED_SCORE)
        top = jnp.max(scores, axis=0, keepdims=True)
        weights = jnp.exp(scores - top)
        top_ref[unit] = top
        total_ref[unit] = jnp.sum(weights, axis=0, keepdims=True)
        added = jnp.dot(kv.T, weights.astype(jnp.bfloat16), preferred_element_type=jnp.float32)
        mix_ref[unit] = added[HD:]

    over_units(diagonal, 0, units)

    def forward(level, part):
        chain(level - 1, part).wait_recv()
        pass_on(level, part)
        across(level, part).start()

    @pl.when(steps.level >= 1)
    def _():
        for part in range(PARTS):
            forward(1, part)

    @pl.when(steps.side == 1)
    def _():
        for part in range(PARTS):
            across(0, part).wait_recv()
            over_units(lambda unit: add(unit, all_ref[ctx - 1, unit]), part * per_part, per_part)

    def level_step(level, unused):
        first = 2 * (steps.level - level)
        for part in range(PARTS):

            @pl.when(level < steps.level)
            def _():
                forward(level + 1, part)

            across(level, part).wait_recv()
            over_units(
                lambda unit: add(unit, all_ref[pl.ds(first, 2), unit].reshape(2 * keys, deep)),
                part * per_part,
                per_part,
            )

        @pl.when(level == 1)
        def _():
            second_half()

        return unused

    @pl.when(steps.level == 0)
    def _():
        second_half()

    lax.fori_loop(1, steps.level + 1, level_step, 0)

    def close(unit):
        total = total_ref[unit]
        mix_ref[unit] = mix_ref[unit] / total
        log_ref[unit] = top_ref[unit] + jnp.log(total)

    over_units(close, 0, units)
    for sequence in range(sequences):
        for pair in range(H // 2):
            heads = []
            for head in (2 * pair, 2 * pair + 1):
                unit, member = sequence * KVH + head // groups, head % groups
                heads.append(mix_ref[unit, :, member * keys : (member + 1) * keys])
            tile = jnp.concatenate(heads, axis=0).astype(low_ref.dtype)
            block = slice(sequence * keys, (sequence + 1) * keys)
            columns = slice(pair * 2 * HD, (pair + 1) * 2 * HD)
            low_t_ref[columns, block] = tile
            low_ref[block, columns] = tile.T
    for gather, _ in gathers:
        gather.sent()
    for step in range(1, group):
        gain_copy(step).wait_send()
    gathered.to_sibling()
    gathered_g.forward()
    gathered.arrived()
    gathered.sent()
    gathered_g.sibling_here()
    for step in range(1, gathered_g.chips):
        gathered_g.crossed(step)
    gathered_g.sent()
    for copy in slices:
        copy.wait()
    for copy in background:
        copy.wait()

    def sent(level, unused):
        for part in range(PARTS):

            @pl.when(steps.has_above)
            def _():
                chain(level, part).wait_send()

            @pl.when(jnp.logical_or(level > 0, steps.side == 0))
            def _():
                across(level, part).wait_send()

        return unused

    lax.fori_loop(0, steps.level + 1, sent, 0)


ANY = pl.BlockSpec(memory_space=pl.ANY)
VMEM = pl.BlockSpec(memory_space=pltpu.VMEM)


def attend(x, gains, cosine, sine, w_query, w_key, w_value, w_out, w_gate, w_up, g_rows, sequences):
    group, count = lax.axis_size("fsdp"), lax.axis_size("ctx")
    rows, width = x.shape
    own, hidden = w_query.shape[0], w_gate.shape[1] // group
    keys, units, deep = rows // sequences, sequences * KVH, 2 * HD
    wide = H // KVH * keys
    kv_width = KVH * HD
    dma = pltpu.SemaphoreType.DMA
    bf16, f32 = jnp.bfloat16, jnp.float32
    pieces = 2 + width // kv_width
    return pl.pallas_call(
        attend_kernel,
        out_shape=[
            jax.ShapeDtypeStruct((units, deep, wide), bf16),
            jax.ShapeDtypeStruct((width, rows), bf16),
            jax.ShapeDtypeStruct((gains.shape[0], width), f32),
            jax.ShapeDtypeStruct((width, width), bf16),
            jax.ShapeDtypeStruct((width, kv_width), bf16),
            jax.ShapeDtypeStruct((width, kv_width), bf16),
            jax.ShapeDtypeStruct((rows, width), bf16),
            jax.ShapeDtypeStruct((width, rows), bf16),
            jax.ShapeDtypeStruct((units, HD, wide), f32),
            jax.ShapeDtypeStruct((units, 1, wide), f32),
            jax.ShapeDtypeStruct((count, units, keys, deep), bf16),
            jax.ShapeDtypeStruct((width, width), bf16),
            jax.ShapeDtypeStruct((width, hidden), bf16),
            jax.ShapeDtypeStruct((width, hidden), bf16),
            jax.ShapeDtypeStruct((group, rows, width), bf16),
        ],
        in_specs=[VMEM] * 4 + [ANY] * 7,
        out_specs=[VMEM] * 11 + [ANY] * 4,
        scratch_shapes=[
            pltpu.VMEM((rows, width), bf16),
            pltpu.VMEM((rows, kv_width), f32),
            pltpu.VMEM((group,) + gains.shape, f32),
            pltpu.VMEM((own, width), bf16),
            pltpu.VMEM((own, hidden), bf16),
            pltpu.VMEM((own, hidden), bf16),
            pltpu.VMEM((rows, width), bf16),
            pltpu.VMEM((units, 1, wide), f32),
            pltpu.VMEM((units, 1, wide), f32),
            dma((count // 2, PARTS)),
            dma((count // 2 + 1, PARTS)),
            dma((count // 2, PARTS)),
            dma((count // 2, PARTS)),
            half_semaphores(pieces),
            half_semaphores(pieces),
            *[dma((group - 1,))] * 2,
            *[half_semaphores(1)] * 2,
            *[group_semaphores()] * 2,
            *[dma((2, group - 1))] * 2,
            dma((7,)),
        ],
        compiler_params=pltpu.CompilerParams(
            collective_id=1, has_side_effects=True, vmem_limit_bytes=60 << 20
        ),
    )(x, gains, cosine, sine, w_query, w_key, w_value, w_out, w_gate, w_up, g_rows)


class Ring:
    def __init__(self, work, landing, total, semaphores, forward, exchange=False):
        self.fsdp, self.ctx = lax.axis_index("fsdp"), lax.axis_index("ctx")
        self.group, self.count = lax.axis_size("fsdp"), lax.axis_size("ctx")
        self.work, self.landing, self.total = work, landing, total
        self.sends, self.arrivals = semaphores[:2]
        self.part_sends, self.part_arrivals, self.own_sem = semaphores[2:] if exchange else (None,) * 3
        self.exchange = exchange
        side = 0 if forward else 1
        self.place = ring_place(self.ctx, side, self.count)
        self.after = (self.fsdp, ring_ctx(lax.rem(self.place + 1, self.count), side, self.count))
        self.ticks = 2 * self.count - 2 + int(exchange)

    def chunk(self, held, index):
        if self.exchange:
            return held.at[index]
        per = held.shape[0] // self.count
        return held.at[pl.ds(index * per, per)]

    def summing(self, step, index):
        return self.copy(self.chunk(self.work, index), self.landing.at[step], step)

    def handing(self, step, index):
        held = self.chunk(self.total, index)
        return self.copy(held, held, step)

    def copy(self, source, target, step):
        return pltpu.make_async_remote_copy(
            src_ref=source,
            dst_ref=target,
            send_sem=self.sends.at[step],
            recv_sem=self.arrivals.at[step],
            device_id=self.after,
            device_id_type=MESH,
        )

    def part(self, index, step):
        peer = lax.rem(self.fsdp + step, self.group)
        return pltpu.make_async_remote_copy(
            src_ref=self.work.at[index, peer],
            dst_ref=self.total.at[index, self.fsdp],
            send_sem=self.part_sends.at[step - 1],
            recv_sem=self.part_arrivals.at[step - 1],
            device_id=(peer, self.ctx),
            device_id_type=MESH,
        )

    def own_part(self, index):
        return pltpu.make_async_copy(
            self.work.at[index, self.fsdp], self.total.at[index, self.fsdp], self.own_sem
        )

    def start(self):
        self.summing(0, self.place).start()

    def tick(self, at):
        last = self.count - 2
        gap = int(self.exchange)
        step = at - gap * jnp.where(at > last, 1, 0) if self.exchange else at
        index = lax.rem(self.place + 3 * self.count - 1 - step, self.count)

        def add(target):
            part, landed = self.chunk(self.work, index), self.landing.at[jnp.minimum(at, last)]
            for row in range(part.shape[0]):
                target[row] = (
                    part[row].astype(jnp.float32) + landed[row].astype(jnp.float32)
                ).astype(part.dtype)

        @pl.when(at <= last)
        def _():
            self.summing(jnp.minimum(at, last), index).wait_recv()

        @pl.when(at < last)
        def _():
            add(self.chunk(self.work, index))
            self.summing(jnp.minimum(at + 1, last), index).start()

        if self.exchange:

            @pl.when(at == last)
            def _():
                add(self.chunk(self.work, index))
                for peer in range(1, self.group):
                    self.part(index, peer).start()
                self.own_part(index).start()

            @pl.when(at == last + 1)
            def _():
                done = lax.rem(self.place + 1, self.count)
                self.own_part(done).wait()
                for peer in range(1, self.group):
                    self.part(done, peer).wait_recv()
                self.handing(last + 1, done).start()

        else:

            @pl.when(at == last)
            def _():
                add(self.chunk(self.total, index))
                self.handing(last + 1, index).start()

        @pl.when(at > last + gap)
        def _():
            here = jnp.maximum(step, last + 1)
            self.handing(here, index).wait_recv()

            @pl.when(here < 2 * self.count - 3)
            def _():
                self.handing(jnp.minimum(here + 1, 2 * self.count - 3), index).start()

    def finish(self):
        def wait(step, unused):
            self.handing(step, self.place).wait_send()
            return unused

        lax.fori_loop(0, 2 * self.count - 2, wait, 0)
        if self.exchange:
            for peer in range(1, self.group):
                self.part(lax.rem(self.place + 1, self.count), peer).wait_send()


class SumRing(Ring):
    def __init__(self, *args):
        super().__init__(*args)
        self.ticks = self.count - 1

    def tick(self, at):
        last = self.count - 2
        index = lax.rem(self.place + 2 * self.count - 1 - at, self.count)
        self.summing(at, index).wait_recv()
        work, landed = self.chunk(self.work, index), self.landing.at[at]

        def add(target):
            for row in range(work.shape[0]):
                target[row] = (
                    work[row].astype(jnp.float32) + landed[row].astype(jnp.float32)
                ).astype(work.dtype)

        @pl.when(at < last)
        def _():
            add(work)
            self.summing(jnp.minimum(at + 1, last), index).start()

        @pl.when(at == last)
        def _():
            add(self.total)

    def finish(self):
        def wait(step, unused):
            self.summing(step, self.place).wait_send()
            return unused

        lax.fori_loop(0, self.ticks, wait, 0)


class SpreadRing(Ring):
    def __init__(self, total, semaphores, forward):
        super().__init__(None, None, total, semaphores, forward)
        self.ticks = self.count - 1
        self.first = lax.rem(self.place + 1, self.count)

    def start(self):
        self.handing(0, self.first).start()

    def tick(self, at):
        index = lax.rem(self.place + self.count - at, self.count)
        self.handing(at, index).wait_recv()

        @pl.when(at < self.count - 2)
        def _():
            self.handing(jnp.minimum(at + 1, self.count - 2), index).start()

    def finish(self):
        def wait(step, unused):
            self.handing(step, self.place).wait_send()
            return unused

        lax.fori_loop(0, self.ticks, wait, 0)


def ring_scratch(chunk, exchange=False):
    count = lax.axis_size("ctx")
    work = (count,) + chunk if exchange else (count * chunk[0],) + chunk[1:]
    return [pltpu.VMEM(work, jnp.bfloat16), pltpu.VMEM((count - 1,) + chunk, jnp.bfloat16)]


def ring_total(chunk, exchange=False):
    count = lax.axis_size("ctx")
    work = (count,) + chunk if exchange else (count * chunk[0],) + chunk[1:]
    return jax.ShapeDtypeStruct(work, jnp.bfloat16)


def ring_semaphores(exchange=False):
    dma, steps = pltpu.SemaphoreType.DMA, 2 * lax.axis_size("ctx") - 2
    parts = lax.axis_size("fsdp") - 1
    return [dma((steps,))] * 2 + ([dma((parts,))] * 2 + [dma] if exchange else [])


def wide_split(width):
    group, count = lax.axis_size("fsdp"), lax.axis_size("ctx")
    return 2 if FF // group // LANES * (width // group // 16) >= 4 * count else 1


def query_split(width):
    return width // LANES * 7 // 9 * LANES


def out_split(width):
    return (width // LANES + 1) // 2 * LANES


def down_split(blocks, count):
    each = -(-blocks // count)
    rings = 4 if each >= 4 else 2
    return [max(1, (each + at) // rings) for at in range(rings)]


class GroupScatter:
    def __init__(self, give_sib, got_sib, give_cross, got_cross, far, got_far, sends, arrivals):
        self.give_sib, self.got_sib = give_sib, got_sib
        self.give_cross, self.got_cross = give_cross, got_cross
        self.far, self.got_far = far, got_far
        self.sends, self.arrivals = sends, arrivals
        self.fsdp, self.ctx = lax.axis_index("fsdp"), lax.axis_index("ctx")
        self.chips = lax.axis_size("fsdp") // 2
        self.chip, self.core = lax.div(self.fsdp, 2), lax.rem(self.fsdp, 2)
        self.sibling = 2 * self.chip + 1 - self.core

    def copy(self, source, target, semaphore, device):
        return pltpu.make_async_remote_copy(
            src_ref=source,
            dst_ref=target,
            send_sem=self.sends.at[semaphore],
            recv_sem=self.arrivals.at[semaphore],
            device_id=(device, self.ctx),
            device_id_type=MESH,
        )

    def to_sibling(self):
        return self.copy(self.give_sib, self.got_sib, 0, self.sibling)

    def to_cross(self, step):
        return self.copy(
            self.give_cross(step), self.got_cross.at[step - 1], step, self.sibling
        )

    def to_far(self, step):
        chip = lax.rem(self.chip + self.chips - step, self.chips)
        return self.copy(
            self.far.at[step - 1],
            self.got_far.at[step - 1],
            self.chips - 1 + step,
            2 * chip + self.core,
        )

    def add_cross(self, step):
        self.to_cross(step).wait_recv()
        held = self.far.at[step - 1]
        held[...] = (
            held[...].astype(jnp.float32) + self.got_cross[step - 1].astype(jnp.float32)
        ).astype(held.dtype)
        self.to_far(step).start()

    def total(self, own):
        self.to_sibling().wait_recv()
        value = own + self.got_sib[...].astype(jnp.float32)
        for step in range(1, self.chips):
            self.to_far(step).wait_recv()
            value = value + self.got_far[step - 1].astype(jnp.float32)
        return value

    def sent(self):
        self.to_sibling().wait_send()
        for step in range(1, self.chips):
            self.to_cross(step).wait_send()
            self.to_far(step).wait_send()


def scatter_scratch(rows, width):
    far = lax.axis_size("fsdp") // 2 - 1
    one, many = (rows, width), (far, rows, width)
    return [pltpu.VMEM(shape, jnp.bfloat16) for shape in (one, one, many, many, many, many)]


def dot_columns(left, right):
    return lax.dot_general(
        left, right, (((1,), (1,)), ((), ())), preferred_element_type=jnp.float32
    )


def tiles(count, body):
    def step(at, unused):
        body(at)
        return unused

    lax.fori_loop(0, count, step, 0)


def lane_tile(at, size):
    return pl.ds(pl.multiple_of(at * size, LANES), size)


def width_tile(width):
    return 384 if width % 384 == 0 else width


def hidden_tile(hidden):
    return 256 if hidden % 256 == 0 else 128


def transpose_into(target, source):
    rows, columns = source.shape

    def body(at):
        part = source[:, lane_tile(at, LANES)]
        target[pl.ds(pl.multiple_of(at * LANES, LANES), LANES), :] = part.T

    tiles(columns // LANES, body)


def ffn_kernel(
    x_ref, low_ref, out_ref, gain_ref, gate_in, up_in, down_in, all_g_in,
    layer_ref, resid_grad_ref, branch_ref, g_wide_ref, gate_part_out, up_part_out, layer_part_out,
    *rest,
):
    downs = len(down_split(gate_in.shape[1] // 16, lax.axis_size("ctx")))
    taken = iter(rest)

    def take(number):
        return [next(taken) for _ in range(number)]

    down_done, (gain_grad_ref,) = take(downs), take(1)
    all_n_ref, turned_n, turned_act, act_ref, gate_grad, up_grad, resid_ref, grad_own = take(8)
    down_scratch = take(2 * downs)
    give_sib, got_sib, give_cross, got_cross, far, got_far = take(6)
    n_sends, n_arrivals, grad_sends, grad_arrivals = take(4)
    gate_ref, up_ref, down_ref, all_g_ref, gate_part_ref, up_part_ref, layer_part_ref = take(7)
    (local_sems,) = take(1)
    loads = [
        pltpu.make_async_copy(source, target, local_sems.at[at])
        for at, (source, target) in enumerate(
            ((gate_in, gate_ref), (up_in, up_ref), (all_g_in, all_g_ref), (down_in, down_ref))
        )
    ]
    for copy in loads:
        copy.start()
    stores = []

    def store(source, target):
        copy = pltpu.make_async_copy(source, target, local_sems.at[len(loads) + len(stores)])
        copy.start()
        stores.append(copy)

    rings = [
        SumRing(*down_scratch[2 * at : 2 * at + 2], down_done[at], take(2), at % 2 == 0)
        for at in range(downs)
    ]
    group = lax.axis_size("fsdp")
    rows, width = x_ref.shape
    hidden = gate_ref.shape[1]
    barrier = pltpu.get_barrier_semaphore()
    greeted = greet_group(barrier) + 2
    for ring in rings[:2]:
        pl.semaphore_signal(barrier, inc=1, device_id=ring.after, device_id_type=MESH)
    step_in, step_out = hidden_tile(hidden), width_tile(width)

    def branch(at):
        columns = lane_tile(at, step_out)
        resid_ref[:, columns] = x_ref[:, columns].astype(jnp.float32) + forward_dot(
            low_ref[...], out_ref[:, columns]
        )

    tiles(width // step_out, branch)
    gain = gain_ref[...]
    scale = norm_scale(resid_ref[...])
    gathered = GroupGather(lambda shard: all_n_ref.at[shard], n_sends, n_arrivals)
    fsdp, chips = gathered.fsdp, gathered.chips
    all_n_ref[fsdp] = (resid_ref[...] * scale * gain).astype(jnp.bfloat16)
    pl.semaphore_wait(barrier, greeted)
    gathered.start(all_n_ref.at[fsdp])
    grad_sum = GroupScatter(
        give_sib,
        got_sib,
        lambda step: give_cross.at[step - 1],
        got_cross,
        far,
        got_far,
        grad_sends,
        grad_arrivals,
    )

    def hidden_part(shard):
        def body(at):
            columns = lane_tile(at, step_in)
            normed = all_n_ref[shard]
            gate = forward_dot(normed, gate_ref[:, columns])
            upward = forward_dot(normed, up_ref[:, columns])
            grad_act = dot_columns(
                all_g_ref[shard], down_ref[pl.ds(pl.multiple_of(at * step_in, LANES), step_in), :]
            )
            sigmoid = jax.nn.sigmoid(gate)
            silu = gate * sigmoid
            act_ref[shard, :, columns] = (silu * upward).astype(jnp.bfloat16)
            gate_grad[shard, :, columns] = (
                grad_act * upward * (sigmoid * (1.0 + gate * (1.0 - sigmoid)))
            ).astype(jnp.bfloat16)
            up_grad[shard, :, columns] = (grad_act * silu).astype(jnp.bfloat16)

        tiles(hidden // step_in, body)

    def grad_part(shard, target):
        def body(at):
            columns = pl.ds(pl.multiple_of(at * step_out, LANES), step_out)
            target[:, columns] = (
                dot_columns(gate_grad[shard], gate_ref[columns, :])
                + dot_columns(up_grad[shard], up_ref[columns, :])
            ).astype(target.dtype)

        tiles(width // step_out, body)

    for copy in loads:
        copy.wait()
    hidden_part(fsdp)
    gathered.sibling_here()
    sibling = gathered.sibling
    hidden_part(sibling)
    grad_part(sibling, grad_sum.give_sib)
    grad_sum.to_sibling().start()
    gathered.forward()
    grad_part(fsdp, grad_own)
    def turn_act(shard):
        transpose_into(turned_act.at[:, lane_tile(shard, rows)], act_ref.at[shard])

    turn_act(fsdp)
    turn_act(sibling)
    far_shards = []
    for step in range(1, chips):
        ours = gathered.same_core(chips - step)
        theirs = ours + sibling - fsdp
        far_shards.append((step, ours, theirs))
        gathered.crossed(step)
        hidden_part(theirs)
        hidden_part(ours)
        turn_act(theirs)
        turn_act(ours)
    blocks = hidden // 16
    spans, first = [], 0
    for ring in rings:
        last = min(blocks, first + ring.work.shape[0])
        spans.append((first, last, ring.work))
        first = last

    def down_tile(at):
        columns = lane_tile(at, step_out)
        part = forward_dot(
            turned_act[...], all_g_ref[:, :, columns].reshape(group * rows, step_out)
        ).astype(jnp.bfloat16)
        for begin, end, work in spans:
            if end > begin:
                work[: end - begin, :, columns] = part[begin * 16 : end * 16].reshape(
                    end - begin, 16, step_out
                )

    tiles(width // step_out, down_tile)
    for begin, end, work in spans:
        for spare in range(end - begin, work.shape[0]):
            work[spare] = jnp.zeros(work.shape[1:], work.dtype)
    for ring in rings:
        ring.start()
    for step, ours, theirs in far_shards:
        grad_part(theirs, give_cross.at[step - 1])
        grad_sum.to_cross(step).start()
        grad_part(ours, far.at[step - 1])
        grad_sum.add_cross(step)
    ticked = [0]

    def ring_tick(at):
        for ring in rings:

            @pl.when(at < ring.ticks)
            def _():
                ring.tick(jnp.minimum(at, ring.ticks - 1))

    def ticking(times, body):
        begin = ticked[0]

        def step(at):
            body(at)
            ring_tick(begin + at)

        tiles(times, step)
        ticked[0] += times

    for shard in range(group):
        span = slice(shard * rows, (shard + 1) * rows)
        transpose_into(turned_n.at[:, span], all_n_ref.at[shard])
    own = width // group
    row_blocks = own // 16
    for source, target in ((gate_grad, gate_part_ref), (up_grad, up_part_ref)):

        def weight_tile(at):
            columns = lane_tile(at, step_in)
            part = forward_dot(
                turned_n[...], source[:, :, columns].reshape(group * rows, step_in)
            ).astype(jnp.bfloat16)
            for block in range(step_in // LANES):
                first = (at * (step_in // LANES) + block) * row_blocks
                for owner in range(group):
                    target[owner, pl.ds(first, row_blocks)] = part[
                        owner * own : (owner + 1) * own, block * LANES : (block + 1) * LANES
                    ].reshape(row_blocks, 16, LANES)

        ticking(hidden // step_in, weight_tile)
        filled = hidden // LANES * row_blocks
        for spare in range(filled, target.shape[1]):
            for owner in range(group):
                target[owner, spare] = jnp.zeros(target.shape[2:], target.dtype)
        store(target, gate_part_out if source is gate_grad else up_part_out)

    def layer_tile(at):
        columns = lane_tile(at, step_out)
        part = forward_dot(
            act_ref[...].reshape(group * rows, hidden), down_ref[:, columns]
        ).reshape(group, rows, step_out)
        layer_part_ref[:, :, columns] = part.astype(jnp.bfloat16)

    ticking(width // step_out, layer_tile)
    store(layer_part_ref, layer_part_out)
    layer_ref[...] = resid_ref[...] + layer_part_ref[fsdp].astype(jnp.float32)
    upstream = grad_sum.total(grad_own[...])
    resid = resid_ref[...]
    scaled = upstream * gain
    grad_resid = (
        all_g_ref[fsdp].astype(jnp.float32)
        + scale * scaled
        - resid * scale**3 * jnp.mean(scaled * resid, axis=-1, keepdims=True)
    )
    gain_grad_ref[...] = jnp.sum(upstream * resid * scale, axis=0, keepdims=True)
    resid_grad_ref[...] = grad_resid
    branch_ref[...] = grad_resid.astype(jnp.bfloat16)
    units, _, wide = g_wide_ref.shape
    sequences = units // KVH
    keys = rows // sequences
    groups = wide // keys
    g_wide_ref[:, :HD, :] = jnp.zeros((units, HD, wide), g_wide_ref.dtype)
    for pair in range(H // 2):
        columns = slice(pair * 2 * HD, (pair + 1) * 2 * HD)
        mixed = dot_columns(branch_ref[...], out_ref[columns, :]).astype(jnp.bfloat16)
        for sequence in range(sequences):
            turned = mixed[sequence * keys : (sequence + 1) * keys].T
            for half in range(2):
                head = 2 * pair + half
                unit, member = sequence * KVH + head // groups, head % groups
                g_wide_ref[unit, HD:, member * keys : (member + 1) * keys] = turned[
                    half * HD : (half + 1) * HD
                ]
    begin = ticked[0]
    tiles(max(0, rings[0].ticks - begin), lambda at: ring_tick(begin + at))
    gathered.sent()
    grad_sum.sent()
    for ring in rings:
        ring.finish()
    for copy in stores:
        copy.wait()


def spread(blocks, count):
    return -(-blocks // count) * count


def feed_forward(x, low, full_out, my_gate, my_up, my_down, all_g, gain, units, wide):
    group, count = lax.axis_size("fsdp"), lax.axis_size("ctx")
    rows, width = x.shape
    hidden = my_gate.shape[1]
    blocks = spread(hidden // LANES * (width // group // 16), wide_split(width) * count)
    chips = group // 2
    dma = pltpu.SemaphoreType.DMA((2 * chips - 1,))
    bf16 = jnp.bfloat16
    down_chunks = [(per, 16, width) for per in down_split(hidden // 16, count)]
    return pl.pallas_call(
        ffn_kernel,
        out_shape=[
            jax.ShapeDtypeStruct((rows, width), jnp.float32),
            jax.ShapeDtypeStruct((rows, width), jnp.float32),
            jax.ShapeDtypeStruct((rows, width), bf16),
            jax.ShapeDtypeStruct((units, 2 * HD, wide), bf16),
            jax.ShapeDtypeStruct((group, blocks, 16, LANES), bf16),
            jax.ShapeDtypeStruct((group, blocks, 16, LANES), bf16),
            jax.ShapeDtypeStruct((group, rows, width), bf16),
            *[jax.ShapeDtypeStruct(chunk, bf16) for chunk in down_chunks],
            jax.ShapeDtypeStruct((1, width), jnp.float32),
        ],
        in_specs=[VMEM] * 4 + [ANY] * 4,
        out_specs=[VMEM] * 4 + [ANY] * 3 + [VMEM] * (1 + len(down_chunks)),
        scratch_shapes=[
            pltpu.VMEM((group, rows, width), bf16),
            pltpu.VMEM((width, group * rows), bf16),
            pltpu.VMEM((hidden, group * rows), bf16),
            pltpu.VMEM((group, rows, hidden), bf16),
            pltpu.VMEM((group, rows, hidden), bf16),
            pltpu.VMEM((group, rows, hidden), bf16),
            pltpu.VMEM((rows, width), jnp.float32),
            pltpu.VMEM((rows, width), jnp.float32),
            *[kind for chunk in down_chunks for kind in ring_scratch(chunk)],
            *scatter_scratch(rows, width),
            *[dma] * 4,
            pltpu.VMEM(my_gate.shape, bf16),
            pltpu.VMEM(my_up.shape, bf16),
            pltpu.VMEM(my_down.shape, bf16),
            pltpu.VMEM(all_g.shape, bf16),
            pltpu.VMEM((group, blocks, 16, LANES), bf16),
            pltpu.VMEM((group, blocks, 16, LANES), bf16),
            pltpu.VMEM((group, rows, width), bf16),
            pltpu.SemaphoreType.DMA((7,)),
            *[kind for _ in down_chunks for kind in ring_semaphores()],
        ],
        compiler_params=pltpu.CompilerParams(
            collective_id=2, has_side_effects=True, vmem_limit_bytes=60 << 20
        ),
    )(x, low, full_out, gain, my_gate, my_up, my_down, all_g)


def back_kernel(
    down_blocks, q_ref, g_ref, log_ref, gain_grad_ref, gain_ref, cos_ref, sin_ref,
    pairs_ref, mix_in, gate_ref, up_ref, layer_base_in, layer_part_ref, branch_ref, low_t_ref,
    normed_t_ref, w_query_in, w_key_in, w_value_in, x_in, resid_grad_in, *rest,
):
    taken = iter(rest)

    def take(number):
        return [next(taken) for _ in range(number)]

    halves, downs = wide_split(x_in.shape[1]), len(down_blocks)
    down_refs = take(downs)
    tokens_ref, layer_ref = take(2)
    wide_totals, down_totals = take(2 * halves), take(downs)
    out_a_total, out_b_total, rest_a_total, rest_b_total = take(4)
    peer_got, chain_got, layer_sib, layer_cross, layer_far = take(5)
    kv_ref, stage_ref, final_ref, qg_ref, delta_ref, grad_q_ref = take(6)
    wide_scratch = take(4 * halves)
    out_a_work, out_a_land, out_b_work, out_b_land = take(4)
    rest_a_work, rest_a_land, rest_b_work, rest_b_land = take(4)
    low_all, normed_all, branch_all, query_all, pair_all, upstream_ref, gain_give, gain_got = take(8)
    far_ref, layer_stage = take(2)
    mix_ref, layer_base_ref, w_query_ref, w_key_ref, w_value_ref, x_ref, resid_grad_ref = take(7)
    steps = Steps()
    fsdp, ctx, group, count = steps.fsdp, steps.ctx, lax.axis_size("fsdp"), lax.axis_size("ctx")
    units, deep, wide = q_ref.shape
    keys = pairs_ref.shape[2]
    rows, width = x_ref.shape
    own = width // group
    wide_rings = [
        Ring(*wide_scratch[2 * at : 2 * at + 2], wide_totals[at], take(5), at < halves, True)
        for at in range(2 * halves)
    ]
    down_rings = [SpreadRing(total, take(2), at % 2 == 0) for at, total in enumerate(down_totals)]
    out_a = Ring(out_a_work, out_a_land, out_a_total, take(2), True)
    out_b = Ring(out_b_work, out_b_land, out_b_total, take(2), False)
    layer_sum = GroupScatter(
        None,
        layer_sib,
        lambda step: layer_part_ref.at[
            2 * lax.rem(lax.div(fsdp, 2) + group // 2 - step, group // 2) + 1 - lax.rem(fsdp, 2)
        ],
        layer_cross,
        far_ref,
        layer_far,
        *take(2),
    )
    layer_sum.give_sib = layer_part_ref.at[layer_sum.sibling]
    rest_a = Ring(rest_a_work, rest_a_land, rest_a_total, take(2), True)
    rest_b = Ring(rest_b_work, rest_b_land, rest_b_total, take(2), False)
    first_rings = []
    for at in range(halves):
        first_rings += [wide_rings[at], wide_rings[halves + at]]
        first_rings += down_rings[at * downs // halves : (at + 1) * downs // halves]
    begun_rings = len(first_rings)
    first_rings += [out_a, out_b]
    peer_sends, peer_arrivals, chain_sends, chain_arrivals = take(4)
    branch_gather = GroupGather(lambda shard: branch_all.at[shard], *take(2))
    query_gather = GroupGather(lambda shard: query_all.at[shard], *take(2))
    pair_gather = GroupGather(lambda shard: pair_all.at[shard], *take(2))
    low_sends, low_arrivals, normed_sends, normed_arrivals, gain_sends, gain_arrivals = take(6)
    local_sems, stage_sems = take(2)

    barrier = pltpu.get_barrier_semaphore()
    greeted = steps.greet(barrier) + greet_group(barrier) + 2
    for device in (out_a.after, out_b.after):
        pl.semaphore_signal(barrier, inc=1, device_id=device, device_id_type=MESH)

    loads = []

    def load(source, target):
        copy = pltpu.make_async_copy(source, target, local_sems.at[len(loads)])
        copy.start()
        loads.append(copy)

    n = wide_scratch[0].shape[2]
    for at, ring in enumerate(wide_rings):
        source = (gate_ref, up_ref)[at // halves]
        for chunk in range(count):
            load(source.at[:, pl.ds((at % halves * count + chunk) * n, n)], ring.work.at[chunk])
    for ring, source in zip(down_rings, down_refs):
        load(source, ring.chunk(ring.total, ring.first))
    ring_loads = len(loads)
    load(pairs_ref, kv_ref)
    load(mix_in, mix_ref)
    load(branch_ref, branch_all.at[fsdp])
    load(low_t_ref.at[pl.ds(fsdp * own, own)], low_all.at[:, lane_tile(fsdp, rows)])
    load(normed_t_ref.at[pl.ds(fsdp * own, own)], normed_all.at[:, lane_tile(fsdp, rows)])
    slot_loads = len(loads)
    for source, target in (
        (layer_base_in, layer_base_ref),
        (w_query_in, w_query_ref),
        (w_key_in, w_key_ref),
        (w_value_in, w_value_ref),
        (x_in, x_ref),
        (resid_grad_in, resid_grad_ref),
    ):
        load(source, target)
    for copy in loads[:ring_loads]:
        copy.wait()
    pl.semaphore_wait(barrier, greeted)
    for ring in first_rings[:begun_rings]:
        ring.start()
    branch_gather.start(branch_ref)
    layer_sum.to_sibling().start()
    for step in range(1, group // 2):
        layer_sum.to_cross(step).start()

    def slices(source, target, sends, arrivals, step):
        peer = lax.rem(fsdp + step, group)
        return pltpu.make_async_remote_copy(
            src_ref=source.at[pl.ds(peer * own, own)],
            dst_ref=target.at[:, lane_tile(fsdp, rows)],
            send_sem=sends.at[step - 1],
            recv_sem=arrivals.at[step - 1],
            device_id=(peer, ctx),
            device_id_type=MESH,
        )

    turned = [
        slices(*ends, step)
        for ends in (
            (low_t_ref, low_all, low_sends, low_arrivals),
            (normed_t_ref, normed_all, normed_sends, normed_arrivals),
        )
        for step in range(1, group)
    ]
    for copy in turned:
        copy.start()

    def prepare(unit):
        q, g = q_ref[unit], g_ref[unit]
        qg_ref[unit, :wide] = q.T
        qg_ref[unit, wide:] = g.T
        delta_ref[unit] = jnp.sum(
            g[HD:].astype(jnp.float32) * mix_ref[unit], axis=0, keepdims=True
        )
        grad_q_ref[unit] = jnp.zeros((HD, wide), jnp.float32)

    for copy in loads[ring_loads:slot_loads]:
        copy.wait()
    tiles(units, prepare)

    def tick(ring, at):
        @pl.when(jnp.logical_and(at >= 0, at < ring.ticks))
        def _():
            ring.tick(jnp.clip(at, 0, ring.ticks - 1))

    late = steps.levels // 2 + 1

    def pump(at):
        lag = [0] * begun_rings + [late, late]
        for turn, ring in enumerate(first_rings):

            @pl.when(lax.rem(at, len(first_rings)) == turn)
            def _():
                tick(ring, lax.div(at, len(first_rings)) - lag[turn])

    def back(unit, first, blocks, diagonal):
        kv = kv_ref[pl.ds(first, blocks), unit].reshape(blocks * keys, deep)
        scores = jnp.dot(kv, q_ref[unit], preferred_element_type=jnp.float32)
        probs = jnp.exp(scores - log_ref[unit])
        if diagonal:
            probs = jnp.where(causal(keys, wide, scores.shape), probs, 0.0)
        grad_probs = jnp.dot(kv, g_ref[unit], preferred_element_type=jnp.float32)
        grad_scores = (probs * (grad_probs - delta_ref[unit])).astype(jnp.bfloat16)
        both = jnp.concatenate([grad_scores, probs.astype(jnp.bfloat16)], axis=1)
        grad_kv = jnp.dot(both, qg_ref[unit], preferred_element_type=jnp.float32)
        added = jnp.dot(kv.T, grad_scores, preferred_element_type=jnp.float32)
        grad_q_ref[unit] = grad_q_ref[unit] + added[:HD]
        kv_ref[pl.ds(first, blocks), unit] = grad_kv.astype(kv_ref.dtype).reshape(
            blocks, keys, deep
        )

    def across(pair):
        return pltpu.make_async_remote_copy(
            src_ref=kv_ref.at[2 * pair + 1 - steps.side],
            dst_ref=peer_got.at[pair],
            send_sem=peer_sends.at[pair],
            recv_sem=peer_arrivals.at[pair],
            device_id=steps.peer,
            device_id_type=MESH,
        )

    def down_chain(pair):
        return pltpu.make_async_remote_copy(
            src_ref=kv_ref.at[2 * pair + steps.side],
            dst_ref=chain_got.at[pair],
            send_sem=chain_sends.at[pair],
            recv_sem=chain_arrivals.at[pair],
            device_id=steps.below,
            device_id_type=MESH,
        )

    def combine(time):
        pair = time - steps.levels + steps.level

        @pl.when(jnp.logical_and(pair >= 0, pair <= steps.level))
        def _():
            for slot, expected, arrival, source in (
                (0, jnp.logical_or(pair < steps.level, steps.side == 0), across, peer_got),
                (1, steps.has_above, down_chain, chain_got),
            ):

                @pl.when(expected)
                def _():
                    arrival(pair).wait_recv()
                    copy = pltpu.make_async_copy(
                        source.at[pair], stage_ref.at[slot], stage_sems.at[slot]
                    )
                    copy.start()
                    copy.wait()

                @pl.when(jnp.logical_not(expected))
                def _():
                    stage_ref[slot] = jnp.zeros(stage_ref.shape[1:], stage_ref.dtype)

            def add(unit):
                final_ref[unit] = (
                    kv_ref[2 * pair + steps.side, unit].astype(jnp.float32)
                    + stage_ref[0, unit].astype(jnp.float32)
                    + stage_ref[1, unit].astype(jnp.float32)
                )

            tiles(units, add)

            @pl.when(pair < steps.level)
            def _():
                kv_ref[2 * pair + steps.side] = final_ref[...].astype(kv_ref.dtype)
                down_chain(pair).start()

    row_blocks = own // 16

    def weight_grad(left, right, begin, end, target, first, loop):
        span = LANES * next(n for n in (3, 2, 1) if (end - begin) % (n * LANES) == 0)

        def body(at):
            columns = pl.ds(pl.multiple_of(begin + at * span, LANES), span)
            part = forward_dot(
                left[...], right[:, :, columns].reshape(group * rows, span)
            ).astype(jnp.bfloat16)
            for block in range(span // LANES):
                here = first + (at * (span // LANES) + block) * row_blocks
                target[pl.ds(here, row_blocks)] = part[
                    :, block * LANES : (block + 1) * LANES
                ].reshape(row_blocks, 16, LANES)

        loop((end - begin) // span, body)
        return first + (end - begin) // LANES * row_blocks

    def clear_from(target, first):
        for spare in range(first, target.shape[0]):
            target[spare] = jnp.zeros((16, LANES), jnp.bfloat16)

    def out_grad():
        for copy in turned[: group - 1]:
            copy.wait_recv()
        branch_gather.forward()
        branch_gather.sibling_here()
        for step in range(1, branch_gather.chips):
            branch_gather.crossed(step)
        split = out_split(width)
        clear_from(out_a_work, weight_grad(low_all, branch_all, 0, split, out_a_work, 0, tiles))
        clear_from(out_b_work, weight_grad(low_all, branch_all, split, width, out_b_work, 0, tiles))
        out_a.start()
        out_b.start()

    turns = units // 2
    rings = max(turns, len(first_rings))

    def slot(pair):
        def turn(at):
            @pl.when(jnp.logical_and(pair < steps.level, at < turns))
            def _():
                for unit in (2 * at, 2 * at + 1):
                    back(unit, 2 * pair, 2, False)

            @pl.when(jnp.logical_and(pair == steps.level, at < turns))
            def _():
                for unit in (2 * at, 2 * at + 1):
                    back(unit, ctx, 1, True)

            @pl.when((pair == steps.level) & (steps.side == 1) & (at < turns))
            def _():
                for unit in (2 * at, 2 * at + 1):
                    back(unit, ctx - 1, 1, False)

            pump(pair * rings + at)

        tiles(rings, turn)

        @pl.when(jnp.logical_or(pair < steps.level, (pair == steps.level) & (steps.side == 1)))
        def _():
            across(pair).start()

        combine(pair)

        @pl.when(pair == late - 1)
        def _():
            out_grad()

    tiles(steps.levels, slot)
    pumped = [steps.levels * rings]

    def pump_next(times=1):
        def body(at, unused, begin=pumped[0]):
            pump(begin + at)
            return unused

        lax.fori_loop(0, times, body, 0)
        pumped[0] += times

    def pumping(times, body):
        begin = pumped[0]

        def step(at):
            body(at)
            tiles(2, lambda more: pump(begin + 2 * at + more))

        tiles(times, step)
        pumped[0] += 2 * times

    cosine, sine = cos_ref[...], sin_ref[...]

    def unturn(columns):
        first, second = columns[: HD // 2], columns[HD // 2 :]
        return jnp.concatenate(
            [first * cosine + second * sine, second * cosine - first * sine], axis=0
        )

    sequences = units // KVH
    groups = wide // keys
    for sequence in range(sequences):
        span = slice(sequence * keys, (sequence + 1) * keys)
        for pair in range(H // 2):
            heads = []
            for head in (2 * pair, 2 * pair + 1):
                unit, member = sequence * KVH + head // groups, head % groups
                part = grad_q_ref[unit, :, member * keys : (member + 1) * keys]
                heads.append(unturn(part * HD ** (-0.5)))
            query_all[fsdp, span, pair * 2 * HD : (pair + 1) * 2 * HD] = (
                jnp.concatenate(heads, axis=0).astype(jnp.bfloat16).T
            )
        pump_next(3)
    query_gather.start(query_all.at[fsdp])
    combine(steps.levels)
    kv_width = KVH * HD
    for sequence in range(sequences):
        span = slice(sequence * keys, (sequence + 1) * keys)
        for pair in range(KVH // 2):
            turned_keys, turned_values = [], []
            for unit in (sequence * KVH + 2 * pair, sequence * KVH + 2 * pair + 1):
                part = final_ref[unit].T
                turned_keys.append(unturn(part[:HD]))
                turned_values.append(part[HD:])
            for start, parts in ((0, turned_keys), (kv_width, turned_values)):
                pair_all[fsdp, span, start + pair * 2 * HD : start + (pair + 1) * 2 * HD] = (
                    jnp.concatenate(parts, axis=0).astype(jnp.bfloat16).T
                )
    pair_gather.start(pair_all.at[fsdp])
    pump_next(2)
    query_gather.forward()
    step_out = width_tile(width)

    def upstream_tile(at):
        columns = pl.ds(pl.multiple_of(at * step_out, LANES), step_out)
        upstream_ref[:, columns] = (
            dot_columns(query_all[fsdp], w_query_ref[columns, :])
            + dot_columns(pair_all[fsdp, :, :kv_width], w_key_ref[columns, :])
            + dot_columns(pair_all[fsdp, :, kv_width:], w_value_ref[columns, :])
        )

    for copy in loads[slot_loads:]:
        copy.wait()
    pumping(width // step_out, upstream_tile)
    inputs = x_ref[...].astype(jnp.float32)
    scale = norm_scale(inputs)
    upstream = upstream_ref[...]
    scaled = upstream * gain_ref[...]
    tokens_ref[...] = (
        resid_grad_ref[...]
        + scale * scaled
        - inputs * scale**3 * jnp.mean(scaled * inputs, axis=-1, keepdims=True)
    )
    gain_attn = jnp.sum(upstream * inputs * scale, axis=0, keepdims=True)
    lanes = width // LANES
    gain_give[...] = jnp.zeros(gain_give.shape, jnp.float32)
    for block in range(lanes):
        columns = slice(block * LANES, (block + 1) * LANES)
        gain_give[block : block + 1, :] = gain_attn[:, columns]
        gain_give[lanes + block : lanes + block + 1, :] = gain_grad_ref[:, columns]

    def gain_copy(step):
        peer = lax.rem(fsdp + step, group)
        return pltpu.make_async_remote_copy(
            src_ref=gain_give,
            dst_ref=gain_got.at[step - 1],
            send_sem=gain_sends.at[step - 1],
            recv_sem=gain_arrivals.at[step - 1],
            device_id=(peer, ctx),
            device_id_type=MESH,
        )

    for step in range(1, group):
        gain_copy(step).start()
    pump_next()
    for copy in turned[group - 1 :]:
        copy.wait_recv()
    query_gather.sibling_here()
    for step in range(1, query_gather.chips):
        query_gather.crossed(step)
    split = query_split(width)
    filled_a = weight_grad(normed_all, query_all, 0, split, rest_a_work, 0, pumping)
    filled_b = weight_grad(normed_all, query_all, split, width, rest_b_work, 0, pumping)
    pair_gather.forward()
    pump_next()
    pair_gather.sibling_here()
    for step in range(1, pair_gather.chips):
        pair_gather.crossed(step)
    filled_b = weight_grad(normed_all, pair_all, 0, 2 * kv_width, rest_b_work, filled_b, pumping)
    for step in range(1, layer_sum.chips):
        ours = layer_part_ref.at[2 * lax.rem(layer_sum.chip + layer_sum.chips - step, layer_sum.chips) + layer_sum.core]
        for source, target in ((ours, far_ref.at[step - 1]), (layer_cross.at[step - 1], layer_stage)):
            if source is not ours:
                layer_sum.to_cross(step).wait_recv()
            copy = pltpu.make_async_copy(source, target, stage_sems.at[0])
            copy.start()
            copy.wait()
        far_ref[step - 1] = (
            far_ref[step - 1].astype(jnp.float32) + layer_stage[...].astype(jnp.float32)
        ).astype(jnp.bfloat16)
        layer_sum.to_far(step).start()
    gains = gain_give[...]
    for step in range(1, group):
        gain_copy(step).wait_recv()
        gains = gains + gain_got[step - 1]
    gain_tiles = gains.shape[0] // 16
    rest_a_work[filled_a : filled_a + gain_tiles] = gains.astype(jnp.bfloat16).reshape(
        gain_tiles, 16, LANES
    )
    clear_from(rest_a_work, filled_a + gain_tiles)
    clear_from(rest_b_work, filled_b)
    rest_a.start()
    rest_b.start()
    begun = pumped[0]
    total_pumps = max(wide_rings[0].ticks, late + out_a.ticks) * len(first_rings)

    half = -(-(total_pumps - begun) // rest_a.ticks)

    def layer_close():
        layer_sum.to_sibling().wait_recv()
        arrived = [layer_sib]
        for step in range(1, layer_sum.chips):
            layer_sum.to_far(step).wait_recv()
            arrived.append(layer_far.at[step - 1])
        for source in arrived:
            copy = pltpu.make_async_copy(source, layer_stage, stage_sems.at[0])
            copy.start()
            copy.wait()

            def add(at):
                block = pl.ds(pl.multiple_of(at * 32, 32), 32)
                layer_base_ref[block] = layer_base_ref[block] + layer_stage[block].astype(
                    jnp.float32
                )

            tiles(rows // 32, add)

        def close(at):
            block = pl.ds(pl.multiple_of(at * 32, 32), 32)
            layer_ref[block] = layer_base_ref[block].astype(jnp.bfloat16)

        tiles(rows // 32, close)

    def last_ticks(at, unused):
        tiles(half, lambda turn: pump(jnp.minimum(begun + half * at + turn, total_pumps)))
        tick(rest_a, at)
        tick(rest_b, at)

        @pl.when(at == rest_a.ticks * 3 // 4)
        def _():
            layer_close()

        return unused

    lax.fori_loop(0, rest_a.ticks, last_ticks, 0)
    layer_sum.sent()
    for ring in first_rings + [rest_a, rest_b]:
        ring.finish()
    for copy in turned:
        copy.wait_send()
    for gather in (branch_gather, query_gather, pair_gather):
        gather.sent()
    for step in range(1, group):
        gain_copy(step).wait_send()

    def sent(pair):
        @pl.when(jnp.logical_or(pair < steps.level, steps.side == 1))
        def _():
            across(pair).wait_send()

        @pl.when(pair < steps.level)
        def _():
            down_chain(pair).wait_send()

    tiles(steps.level + 1, sent)


def layer_back(
    q_wide, g_wide, log_total, gain_grad, gain, cosine, sine, all_pairs, mix, gate_part, up_part,
    layer_base, layer_parts, branch, low_t, normed_t, w_query, w_key, w_value, x, resid_grad, downs,
):
    group, count = lax.axis_size("fsdp"), lax.axis_size("ctx")
    units, deep, wide = q_wide.shape
    keys = all_pairs.shape[2]
    rows, width = x.shape
    own, kv_width = width // group, w_key.shape[1]
    bf16, f32 = jnp.bfloat16, jnp.float32
    dma = pltpu.SemaphoreType.DMA
    halves = wide_split(width)
    wide_chunk = (group, gate_part.shape[1] // (halves * count), 16, LANES)
    gain_rows = spread(2 * (width // LANES), 16)
    split, row_blocks = query_split(width), own // 16
    out_first = out_split(width)
    chips = group // 2
    small_chunks = [
        (spread(held, count) // count, 16, LANES)
        for held in (
            out_first // LANES * row_blocks,
            (width - out_first) // LANES * row_blocks,
            split // LANES * row_blocks + gain_rows // 16,
            (width - split + 2 * kv_width) // LANES * row_blocks,
        )
    ]
    levels = count // 2
    loaded = [mix, layer_base, w_query, w_key, w_value, x, resid_grad]
    return pl.pallas_call(
        functools.partial(back_kernel, [part.shape[0] for part in downs]),
        out_shape=[
            jax.ShapeDtypeStruct((rows, width), f32),
            jax.ShapeDtypeStruct((rows, width), bf16),
            *[ring_total(wide_chunk, True)] * (2 * halves),
            *[ring_total(part.shape) for part in downs],
            *[ring_total(chunk) for chunk in small_chunks],
            *[jax.ShapeDtypeStruct((levels, units, keys, deep), bf16)] * 2,
            jax.ShapeDtypeStruct((rows, width), bf16),
            *[jax.ShapeDtypeStruct((chips - 1, rows, width), bf16)] * 2,
        ],
        in_specs=[VMEM] * 7 + [ANY] * (14 + len(downs)),
        out_specs=[VMEM] * (6 + 2 * halves + len(downs)) + [ANY] * 5,
        scratch_shapes=[
            pltpu.VMEM(all_pairs.shape, bf16),
            pltpu.VMEM((2, units, keys, deep), bf16),
            pltpu.VMEM((units, keys, deep), f32),
            pltpu.VMEM((units, 2 * wide, deep), bf16),
            pltpu.VMEM((units, 1, wide), f32),
            pltpu.VMEM((units, HD, wide), f32),
            *[kind for _ in range(2 * halves) for kind in ring_scratch(wide_chunk, True)],
            *[kind for chunk in small_chunks for kind in ring_scratch(chunk)],
            pltpu.VMEM((own, group * rows), bf16),
            pltpu.VMEM((own, group * rows), bf16),
            pltpu.VMEM((group, rows, width), bf16),
            pltpu.VMEM((group, rows, width), bf16),
            pltpu.VMEM((group, rows, 2 * kv_width), bf16),
            pltpu.VMEM((rows, width), f32),
            pltpu.VMEM((gain_rows, LANES), f32),
            pltpu.VMEM((group - 1, gain_rows, LANES), f32),
            pltpu.VMEM((chips - 1, rows, width), bf16),
            pltpu.VMEM((rows, width), bf16),
            *[pltpu.VMEM(array.shape, array.dtype) for array in loaded],
            *[kind for _ in range(2 * halves) for kind in ring_semaphores(True)],
            *[kind for _ in range(len(downs) + 2) for kind in ring_semaphores()],
            *[dma((group - 1,))] * 2,
            *[kind for _ in range(2) for kind in ring_semaphores()],
            *[dma((levels,))] * 4,
            *[group_semaphores()] * 6,
            *[dma((group - 1,))] * 6,
            dma((11 + len(downs) + 2 * halves * count,)),
            dma((2,)),
        ],
        compiler_params=pltpu.CompilerParams(
            collective_id=3, has_side_effects=True, vmem_limit_bytes=62 << 20
        ),
    )(
        q_wide, g_wide, log_total, gain_grad, gain, cosine, sine, all_pairs, mix, gate_part, up_part,
        layer_base, layer_parts, branch, low_t, normed_t, w_query, w_key, w_value, x, resid_grad,
        *downs,
    )


def finish_kernel(halves, downs, *refs):
    wides, refs = refs[: 2 * halves], refs[2 * halves :]
    down_refs, refs = refs[:downs], refs[downs:]
    out_a_ref, out_b_ref, rest_a_ref, rest_b_ref = refs[:4]
    query_grad, key_grad, value_grad, out_grad, gate_grad, up_grad, down_grad = refs[4:]
    rows = gate_grad.shape[0]
    row_blocks = rows // 16
    for sources, target in ((wides[:halves], gate_grad), (wides[halves:], up_grad)):
        held = jnp.concatenate(
            [source[...].reshape((-1,) + source.shape[3:]) for source in sources], axis=0
        )
        for block in range(target.shape[1] // LANES):
            target[:, block * LANES : (block + 1) * LANES] = (
                held[block * row_blocks : (block + 1) * row_blocks]
                .reshape(rows, LANES)
                .astype(jnp.float32)
            )

    @pl.when(pl.program_id(0) == 0)
    def _():
        def unpack(source, first, target, begin, end):
            for block in range(begin, end):
                here = first + (block - begin) * row_blocks
                target[:, block * LANES : (block + 1) * LANES] = (
                    source[here : here + row_blocks].reshape(rows, LANES).astype(jnp.float32)
                )
            return first + (end - begin) * row_blocks

        width, kv_width = query_grad.shape[1], key_grad.shape[1]
        split = query_split(width) // LANES
        middle = out_split(width) // LANES
        unpack(out_a_ref, 0, out_grad, 0, middle)
        unpack(out_b_ref, 0, out_grad, middle, width // LANES)
        unpack(rest_a_ref, 0, query_grad, 0, split)
        at = unpack(rest_b_ref, 0, query_grad, split, width // LANES)
        at = unpack(rest_b_ref, at, key_grad, 0, kv_width // LANES)
        unpack(rest_b_ref, at, value_grad, 0, kv_width // LANES)
        blocks, begin = down_grad.shape[0] // 16, 0
        for source in down_refs:
            end = min(blocks, begin + source.shape[0])
            if end > begin:
                down_grad[begin * 16 : end * 16, :] = (
                    source[: end - begin]
                    .reshape((end - begin) * 16, down_grad.shape[1])
                    .astype(jnp.float32)
                )
            begin = end


def finish(wides, downs, smalls, own, width, kv_width, hidden):
    count, group, n = wides[0].shape[:3]

    def whole(array):
        return pl.BlockSpec(array.shape, lambda part, rank=len(array.shape): (0,) * rank)

    wide = pl.BlockSpec((count, 1, n, 16, LANES), lambda part: (0, part, 0, 0, 0))
    outs = [
        jax.ShapeDtypeStruct((own, columns), jnp.float32)
        for columns in (width, kv_width, kv_width, width, FF, FF)
    ] + [jax.ShapeDtypeStruct((hidden, width), jnp.float32)]
    slice_spec = pl.BlockSpec((own, FF // group), lambda part: (0, part))
    return pl.pallas_call(
        functools.partial(finish_kernel, len(wides) // 2, len(downs)),
        grid=(group,),
        out_shape=outs,
        in_specs=[wide] * len(wides) + [whole(a) for a in (*downs, *smalls)],
        out_specs=[whole(a) for a in outs[:4]] + [slice_spec, slice_spec, whole(outs[6])],
        compiler_params=pltpu.CompilerParams(vmem_limit_bytes=60 << 20),
    )(*wides, *downs, *smalls)


def on_device(
    tokens, w_query, w_key, w_value, w_out, w_gate, w_up, w_down, gain_attn, gain_ffn, cotangent
):
    block_len, seq_count, width = tokens.shape
    rows_count = block_len * seq_count
    kv_width = KVH * HD
    positions = lax.axis_index("ctx") * block_len + jnp.arange(block_len, dtype=jnp.int32)
    freqs = ROTARY_BASE ** (-2.0 * jnp.arange(HD // 2, dtype=jnp.float32) / HD)
    angles = freqs[:, None] * positions.astype(jnp.float32)[None, :]
    cosine, sine = jnp.cos(angles), jnp.sin(angles)
    x_rows = jnp.swapaxes(tokens, 0, 1).reshape(rows_count, width)
    g_rows = jnp.swapaxes(cotangent, 0, 1).reshape(rows_count, width)
    own = gain_attn.shape[0]
    units = seq_count * KVH
    wide = H // KVH * block_len
    own_gains = jnp.pad(
        jnp.stack([gain_attn, gain_ffn]).astype(jnp.float32), ((0, 6), (0, spread(own, LANES) - own))
    )
    (
        q_wide, normed_t, gains, full_query, full_key, full_value, attn_low, low_t, mix_unit, log_total,
        all_pairs, full_out, my_gate, my_up, all_g,
    ) = attend(
        x_rows, own_gains, cosine, sine, w_query, w_key, w_value, w_out, w_gate, w_up, g_rows, seq_count
    )
    layer_base, grad_resid, grad_branch, g_wide, gate_part, up_part, layer_parts, *downs = (
        feed_forward(
            x_rows, attn_low, full_out, my_gate, my_up, w_down, all_g, gains[1:2], units, wide
        )
    )
    downs, gain_term_ffn = downs[:-1], downs[-1]
    grad_tokens, layer_out, *sums = layer_back(
        q_wide, g_wide, log_total, gain_term_ffn, gains[:1], cosine, sine, all_pairs, mix_unit,
        gate_part, up_part, layer_base, layer_parts, grad_branch, low_t, normed_t, full_query,
        full_key, full_value, x_rows, grad_resid, downs,
    )
    wides, sums = sums[: 2 * wide_split(width)], sums[2 * wide_split(width) :]
    smalls = sums[len(downs) : len(downs) + 4]
    filled = query_split(width) // LANES * (own // 16)
    gain_grads = smalls[2][filled:].reshape(-1, LANES)[: 2 * (width // LANES)].reshape(2, width)
    gain_grads = lax.dynamic_slice_in_dim(gain_grads, lax.axis_index("fsdp") * own, own, 1)
    gain_grads = gain_grads.astype(jnp.float32)
    grads = finish(wides, sums[: len(downs)], smalls, own, width, kv_width, w_down.shape[0])
    return (
        jnp.swapaxes(layer_out.reshape(seq_count, block_len, width), 0, 1),
        jnp.swapaxes(grad_tokens.reshape(seq_count, block_len, width), 0, 1),
        *grads,
        gain_grads[0],
        gain_grads[1],
    )


def solution(mesh):
    return jax.shard_map(
        on_device,
        mesh=mesh,
        in_specs=(
            P("ctx", "fsdp", None),
            P("fsdp", None),
            P("fsdp", None),
            P("fsdp", None),
            P("fsdp", None),
            P("fsdp", None),
            P("fsdp", None),
            P("fsdp", None),
            P("fsdp"),
            P("fsdp"),
            P("ctx", "fsdp", None),
        ),
        out_specs=(
            P("ctx", "fsdp", None),
            P("ctx", "fsdp", None),
            P("fsdp", None),
            P("fsdp", None),
            P("fsdp", None),
            P("fsdp", None),
            P("fsdp", None),
            P("fsdp", None),
            P("fsdp", None),
            P("fsdp"),
            P("fsdp"),
        ),
        check_vma=False,
    )
```

profile of v0, /device:TPU:0, one launch (start us, length us, event | category | flops | bytes accessed | tf_op | source)
XLA Modules:
  0.0 353.7 jit_solution(14011593280695663265)
XLA Ops:
  0.7 0.7 stack.9
  1.4 0.7 stack.10
  2.0 0.6 fusion.6.gain_ref
  2.7 0.8 multiply_sine_fusion
  3.4 1.9 copy.22
  5.3 1.9 copy.23
  7.3 86.2 %shard_map.194 = (bf16[12,128,384]{2,1,0:T(8,128)(2,1)}, bf16[1152,256]{1,0:T(8,128)(2,1)}, f32[8,1152]{1,0:T(8,128)}, bf16[1152,1152]{1,0:T(8,128)(2,1)}, bf16[...) custom-call(bf16[256,1152]{1,0:T(8,128)(2,1)} %bitcast.13, ...), custom_call_target="tpu_custom_call" | custom-call | tf_op jit(solution)/shard_map/pallas_call | solution.py:598
  93.5 1.4 fusion.7
  94.9 69.4 %shard_map.195 = (f32[256,1152]{1,0:T(8,128)}, f32[256,1152]{1,0:T(8,128)}, bf16[256,1152]{1,0:T(8,128)(2,1)}, bf16[12,128,384]{2,1,0:T(8,128)(2,1)}, bf16[4,112...) custom-call(bf16[256,1152]{1,0:T(8,128)(2,1)} %bitcast.14, ...), custom_call_target="tpu_custom_call" | custom-call | tf_op jit(solution)/shard_map/pallas_call | solution.py:1226
  164.3 173.7 %shard_map.196 = (f32[256,1152]{1,0:T(8,128)}, bf16[256,1152]{1,0:T(8,128)(2,1)}, bf16[8,4,7,16,128]{4,3,2,1,0:T(8,128)(2,1)}, bf16[8,4,7,16,128]{4,3,2,1,0:T(8,...) custom-call(bf16[12,128,384]{2,1,0:T(8,128)(2,1)} %get-tuple-element, ...), custom_call_target="tpu_custom_call" | custom-call | tf_op jit(solution)/shard_map/pallas_call | solution.py:1805
  338.1 0.0 copy-start
  338.1 2.6 copy.29
  340.7 0.0 copy-done
  340.7 1.9 copy.28
  342.6 0.7 slice.20
  343.3 0.1 dynamic-slice_convert_fusion
  343.4 0.6 slice_reduce_fusion
  344.0 9.5 %shard_map.197 = (f32[288,1152]{1,0:T(8,128)}, f32[288,384]{1,0:T(8,128)}, f32[288,384]{1,0:T(8,128)}, f32[288,1152]{1,0:T(8,128)}, f32[288,3072]{1,0:T(8,128)},...) custom-call(bf16[8,4,7,16,128]{4,3,2,1,0:T(8,128)(2,1)} %get-tuple-element.88.refs_0_, ...), custom_call_target="tpu_custom_call" | custom-call | tf_op jit(solution)/shard_map/pallas_call | solution.py:1920
  (4 shorter events, 0.0 us)
Async XLA Ops:
  338.1 2.6 copy-start
where the time goes:
time: 355 us; the launch traced here: 354 us
  Pallas kernels  339 us (95%)
  local copies, waits for them, and re-layouts  12.5 us (4%)
    pallas_call x1, Pallas kernels, layer_back(): pl.pallas_call(functools.partial(back_kernel, [part.shape[0] for part in...  174 us
    pallas_call x1, Pallas kernels, attend(): pl.pallas_call(attend_kernel, out_shape=[jax.ShapeDtypeStruct((units, dee...  86.2 us
    pallas_call x1, Pallas kernels, feed_forward(): pl.pallas_call(ffn_kernel, out_shape=[jax.ShapeDtypeStruct((rows, width),...  69.4 us
    pallas_call x1, Pallas kernels, finish(): pl.pallas_call(functools.partial(finish_kernel, len(wides) // 2, len(down...  9.51 us

commit v1 on v0

--- a/solution.py
+++ b/solution.py
@@ -258,7 +258,7 @@
 
 def attend_kernel(
     x_ref, gain_ref, cos_ref, sin_ref, query_ref, key_ref, value_ref, out_ref, gate_ref, up_ref, g_ref,
-    q_ref, normed_t_ref, gains_ref, full_query, full_key, full_value,
+    q_ref, normed_t_ref, gain_attn_ref, gain_ffn_ref, full_query, full_key, full_value,
     low_ref, low_t_ref, mix_ref, log_ref, all_ref, full_out_ref, my_gate_ref, my_up_ref, all_g_ref,
     normed_ref, key_rows, gain_all, own_out, own_gate, own_up, own_g,
     top_ref, total_ref, chain_sends, chain_arrivals, peer_sends, peer_arrivals,
@@ -319,7 +319,8 @@
     for step in range(1, group):
         gain_copy(step).wait_recv()
     gains = jnp.concatenate([gain_all[shard][:, :own] for shard in range(group)], axis=1)
-    gains_ref[...] = gains
+    gain_attn_ref[...] = gains[:1]
+    gain_ffn_ref[...] = gains[1:2]
     normed_ref[...] = (inputs * scale * gains[:1]).astype(jnp.bfloat16)
     cosine, sine = cos_ref[...], sin_ref[...]
 
@@ -600,7 +601,8 @@
         out_shape=[
             jax.ShapeDtypeStruct((units, deep, wide), bf16),
             jax.ShapeDtypeStruct((width, rows), bf16),
-            jax.ShapeDtypeStruct((gains.shape[0], width), f32),
+            jax.ShapeDtypeStruct((1, width), f32),
+            jax.ShapeDtypeStruct((1, width), f32),
             jax.ShapeDtypeStruct((width, width), bf16),
             jax.ShapeDtypeStruct((width, kv_width), bf16),
             jax.ShapeDtypeStruct((width, kv_width), bf16),
@@ -615,7 +617,7 @@
             jax.ShapeDtypeStruct((group, rows, width), bf16),
         ],
         in_specs=[VMEM] * 4 + [ANY] * 7,
-        out_specs=[VMEM] * 11 + [ANY] * 4,
+        out_specs=[VMEM] * 12 + [ANY] * 4,
         scratch_shapes=[
             pltpu.VMEM((rows, width), bf16),
             pltpu.VMEM((rows, kv_width), f32),
@@ -1857,74 +1859,115 @@
 
 
 def finish_kernel(halves, downs, *refs):
-    wides, refs = refs[: 2 * halves], refs[2 * halves :]
-    down_refs, refs = refs[:downs], refs[downs:]
-    out_a_ref, out_b_ref, rest_a_ref, rest_b_ref = refs[:4]
-    query_grad, key_grad, value_grad, out_grad, gate_grad, up_grad, down_grad = refs[4:]
-    rows = gate_grad.shape[0]
+    taken = iter(refs)
+
+    def take(number):
+        return [next(taken) for _ in range(number)]
+
+    wides, down_refs, smalls, (rows_ref,) = take(2 * halves), take(downs), take(4), take(1)
+    outs, (tokens_ref,) = take(7), take(1)
+    wide_held, down_held, small_held = take(2 * halves), take(downs), take(4)
+    made, (load_sems, store_sems) = take(7), take(2)
+    sources = [*wides, *down_refs, *smalls]
+    held = [*wide_held, *down_held, *small_held]
+    loads = {}
+    for at, (source, target) in enumerate(zip(sources, held)):
+        loads[id(target)] = pltpu.make_async_copy(source, target, load_sems.at[at])
+        loads[id(target)].start()
+    stores = []
+
+    def store(index, columns=None):
+        source, target = made[index], outs[index]
+        if columns is not None:
+            source, target = source.at[:, columns], target.at[:, columns]
+        copy = pltpu.make_async_copy(source, target, store_sems.at[len(stores)])
+        copy.start()
+        stores.append(copy)
+
+    rows = made[4].shape[0]
     row_blocks = rows // 16
-    for sources, target in ((wides[:halves], gate_grad), (wides[halves:], up_grad)):
-        held = jnp.concatenate(
-            [source[...].reshape((-1,) + source.shape[3:]) for source in sources], axis=0
-        )
-        for block in range(target.shape[1] // LANES):
+    group = wides[0].shape[1]
+
+    def unpack(source, first, index, begin, end):
+        target = made[index]
+        for block in range(begin, end):
+            here = first + (block - begin) * row_blocks
             target[:, block * LANES : (block + 1) * LANES] = (
-                held[block * row_blocks : (block + 1) * row_blocks]
-                .reshape(rows, LANES)
+                source[here : here + row_blocks].reshape(rows, LANES).astype(jnp.float32)
+            )
+        return first + (end - begin) * row_blocks
+
+    for index, parts in ((4, wide_held[:halves]), (5, wide_held[halves:])):
+        for part in parts:
+            loads[id(part)].wait()
+        target = made[index]
+        columns = target.shape[1] // group
+        for owner in range(group):
+            tile_rows = jnp.concatenate(
+                [part[:, owner].reshape((-1,) + part.shape[3:]) for part in parts], axis=0
+            )
+            for block in range(columns // LANES):
+                begin = owner * columns + block * LANES
+                target[:, begin : begin + LANES] = (
+                    tile_rows[block * row_blocks : (block + 1) * row_blocks]
+                    .reshape(rows, LANES)
+                    .astype(jnp.float32)
+                )
+            store(index, pl.ds(owner * columns, columns))
+    down_grad = made[6]
+    blocks, begin = down_grad.shape[0] // 16, 0
+    for source in down_held:
+        loads[id(source)].wait()
+        end = min(blocks, begin + source.shape[0])
+        if end > begin:
+            down_grad[begin * 16 : end * 16, :] = (
+                source[: end - begin]
+                .reshape((end - begin) * 16, down_grad.shape[1])
                 .astype(jnp.float32)
             )
-
-    @pl.when(pl.program_id(0) == 0)
-    def _():
-        def unpack(source, first, target, begin, end):
-            for block in range(begin, end):
-                here = first + (block - begin) * row_blocks
-                target[:, block * LANES : (block + 1) * LANES] = (
-                    source[here : here + row_blocks].reshape(rows, LANES).astype(jnp.float32)
-                )
-            return first + (end - begin) * row_blocks
-
-        width, kv_width = query_grad.shape[1], key_grad.shape[1]
-        split = query_split(width) // LANES
-        middle = out_split(width) // LANES
-        unpack(out_a_ref, 0, out_grad, 0, middle)
-        unpack(out_b_ref, 0, out_grad, middle, width // LANES)
-        unpack(rest_a_ref, 0, query_grad, 0, split)
-        at = unpack(rest_b_ref, 0, query_grad, split, width // LANES)
-        at = unpack(rest_b_ref, at, key_grad, 0, kv_width // LANES)
-        unpack(rest_b_ref, at, value_grad, 0, kv_width // LANES)
-        blocks, begin = down_grad.shape[0] // 16, 0
-        for source in down_refs:
-            end = min(blocks, begin + source.shape[0])
-            if end > begin:
-                down_grad[begin * 16 : end * 16, :] = (
-                    source[: end - begin]
-                    .reshape((end - begin) * 16, down_grad.shape[1])
-                    .astype(jnp.float32)
-                )
-            begin = end
-
-
-def finish(wides, downs, smalls, own, width, kv_width, hidden):
-    count, group, n = wides[0].shape[:3]
-
-    def whole(array):
-        return pl.BlockSpec(array.shape, lambda part, rank=len(array.shape): (0,) * rank)
-
-    wide = pl.BlockSpec((count, 1, n, 16, LANES), lambda part: (0, part, 0, 0, 0))
+        begin = end
+    store(6)
+    for part in small_held:
+        loads[id(part)].wait()
+    out_a, out_b, rest_a, rest_b = small_held
+    lanes, kv_lanes = made[0].shape[1] // LANES, made[1].shape[1] // LANES
+    middle, split = out_split(made[0].shape[1]) // LANES, query_split(made[0].shape[1]) // LANES
+    unpack(out_a, 0, 3, 0, middle)
+    unpack(out_b, 0, 3, middle, lanes)
+    store(3)
+    unpack(rest_a, 0, 0, 0, split)
+    at = unpack(rest_b, 0, 0, split, lanes)
+    store(0)
+    at = unpack(rest_b, at, 1, 0, kv_lanes)
+    store(1)
+    unpack(rest_b, at, 2, 0, kv_lanes)
+    store(2)
+    keys = tokens_ref.shape[0]
+    for sequence in range(tokens_ref.shape[1]):
+        tokens_ref[:, sequence, :] = rows_ref[sequence * keys : (sequence + 1) * keys]
+    for copy in stores:
+        copy.wait()
+
+
+def finish(wides, downs, smalls, token_rows, own, kv_width, hidden, sequences):
+    rows, width = token_rows.shape
+    f32 = jnp.float32
     outs = [
-        jax.ShapeDtypeStruct((own, columns), jnp.float32)
+        jax.ShapeDtypeStruct((own, columns), f32)
         for columns in (width, kv_width, kv_width, width, FF, FF)
-    ] + [jax.ShapeDtypeStruct((hidden, width), jnp.float32)]
-    slice_spec = pl.BlockSpec((own, FF // group), lambda part: (0, part))
+    ] + [jax.ShapeDtypeStruct((hidden, width), f32)]
+    sources = [*wides, *downs, *smalls]
+    dma = pltpu.SemaphoreType.DMA
     return pl.pallas_call(
         functools.partial(finish_kernel, len(wides) // 2, len(downs)),
-        grid=(group,),
-        out_shape=outs,
-        in_specs=[wide] * len(wides) + [whole(a) for a in (*downs, *smalls)],
-        out_specs=[whole(a) for a in outs[:4]] + [slice_spec, slice_spec, whole(outs[6])],
+        out_shape=outs + [jax.ShapeDtypeStruct((rows // sequences, sequences, width), f32)],
+        in_specs=[ANY] * len(sources) + [VMEM],
+        out_specs=[ANY] * len(outs) + [VMEM],
+        scratch_shapes=[pltpu.VMEM(array.shape, array.dtype) for array in sources]
+        + [pltpu.VMEM(out.shape, f32) for out in outs]
+        + [dma((len(sources),)), dma((5 + 2 * wides[0].shape[1],))],
         compiler_params=pltpu.CompilerParams(vmem_limit_bytes=60 << 20),
-    )(*wides, *downs, *smalls)
+    )(*sources, token_rows)
 
 
 def on_device(
@@ -1946,19 +1989,19 @@
         jnp.stack([gain_attn, gain_ffn]).astype(jnp.float32), ((0, 6), (0, spread(own, LANES) - own))
     )
     (
-        q_wide, normed_t, gains, full_query, full_key, full_value, attn_low, low_t, mix_unit, log_total,
+        q_wide, normed_t, full_gain_attn, full_gain_ffn, full_query, full_key, full_value, attn_low, low_t, mix_unit, log_total,
         all_pairs, full_out, my_gate, my_up, all_g,
     ) = attend(
         x_rows, own_gains, cosine, sine, w_query, w_key, w_value, w_out, w_gate, w_up, g_rows, seq_count
     )
     layer_base, grad_resid, grad_branch, g_wide, gate_part, up_part, layer_parts, *downs = (
         feed_forward(
-            x_rows, attn_low, full_out, my_gate, my_up, w_down, all_g, gains[1:2], units, wide
+            x_rows, attn_low, full_out, my_gate, my_up, w_down, all_g, full_gain_ffn, units, wide
         )
     )
     downs, gain_term_ffn = downs[:-1], downs[-1]
     grad_tokens, layer_out, *sums = layer_back(
-        q_wide, g_wide, log_total, gain_term_ffn, gains[:1], cosine, sine, all_pairs, mix_unit,
+        q_wide, g_wide, log_total, gain_term_ffn, full_gain_attn, cosine, sine, all_pairs, mix_unit,
         gate_part, up_part, layer_base, layer_parts, grad_branch, low_t, normed_t, full_query,
         full_key, full_value, x_rows, grad_resid, downs,
     )
@@ -1968,10 +2011,12 @@
     gain_grads = smalls[2][filled:].reshape(-1, LANES)[: 2 * (width // LANES)].reshape(2, width)
     gain_grads = lax.dynamic_slice_in_dim(gain_grads, lax.axis_index("fsdp") * own, own, 1)
     gain_grads = gain_grads.astype(jnp.float32)
-    grads = finish(wides, sums[: len(downs)], smalls, own, width, kv_width, w_down.shape[0])
+    *grads, tokens_grad = finish(
+        wides, sums[: len(downs)], smalls, grad_tokens, own, kv_width, w_down.shape[0], seq_count
+    )
     return (
         jnp.swapaxes(layer_out.reshape(seq_count, block_len, width), 0, 1),
-        jnp.swapaxes(grad_tokens.reshape(seq_count, block_len, width), 0, 1),
+        tokens_grad,
         *grads,
         gain_grads[0],
         gain_grads[1],

time: 355 us -> 350 us (0.986)
  no operation moved by 1% of the time
where the time goes in v1:
time: 350 us; the launch traced here: 349 us
  Pallas kernels  338 us (97%)
  local copies, waits for them, and re-layouts  9.05 us (3%)
    pallas_call x1, Pallas kernels, layer_back(): pl.pallas_call(functools.partial(back_kernel, [part.shape[0] for part in...  173 us
    pallas_call x1, Pallas kernels, attend(): pl.pallas_call(attend_kernel, out_shape=[jax.ShapeDtypeStruct((units, dee...  86.2 us
    pallas_call x1, Pallas kernels, feed_forward(): pl.pallas_call(ffn_kernel, out_shape=[jax.ShapeDtypeStruct((rows, width),...  69.5 us
    pallas_call x1, Pallas kernels, finish(): pl.pallas_call(functools.partial(finish_kernel, len(wides) // 2, len(down...  9.16 us

profile of v1, /device:TPU:0, one launch (start us, length us, event | category | flops | bytes accessed | tf_op | source)
XLA Modules:
  0.0 349.4 jit_solution(3871140881525015253)
XLA Ops:
  0.7 0.7 stack.9
  1.4 0.7 stack.10
  2.0 0.6 fusion.6.gain_ref
  2.7 0.8 multiply_sine_fusion
  3.4 1.9 copy.22
  5.3 1.9 copy.23
  7.3 86.2 %shard_map.194 = (bf16[12,128,384]{2,1,0:T(8,128)(2,1)}, bf16[1152,256]{1,0:T(8,128)(2,1)}, f32[1,1152]{1,0:T(1,128)}, f32[1,1152]{1,0:T(1,128)}, bf16[1152,1152...) custom-call(bf16[256,1152]{1,0:T(8,128)(2,1)} %bitcast.9, ...), custom_call_target="tpu_custom_call" | custom-call | tf_op jit(solution)/shard_map/pallas_call | solution.py:599
  93.5 69.5 %shard_map.195 = (f32[256,1152]{1,0:T(8,128)}, f32[256,1152]{1,0:T(8,128)}, bf16[256,1152]{1,0:T(8,128)(2,1)}, bf16[12,128,384]{2,1,0:T(8,128)(2,1)}, bf16[4,112...) custom-call(bf16[256,1152]{1,0:T(8,128)(2,1)} %bitcast.10, ...), custom_call_target="tpu_custom_call" | custom-call | tf_op jit(solution)/shard_map/pallas_call | solution.py:1228
  162.9 173.3 %shard_map.196 = (f32[256,1152]{1,0:T(8,128)}, bf16[256,1152]{1,0:T(8,128)(2,1)}, bf16[8,4,7,16,128]{4,3,2,1,0:T(8,128)(2,1)}, bf16[8,4,7,16,128]{4,3,2,1,0:T(8,...) custom-call(bf16[12,128,384]{2,1,0:T(8,128)(2,1)} %get-tuple-element, ...), custom_call_target="tpu_custom_call" | custom-call | tf_op jit(solution)/shard_map/pallas_call | solution.py:1807
  336.2 2.5 copy.26
  338.7 0.7 slice.12
  339.4 0.1 dynamic-slice_convert_fusion
  339.5 0.6 slice_reduce_fusion
  340.1 9.2 %shard_map.197 = (f32[288,1152]{1,0:T(8,128)}, f32[288,384]{1,0:T(8,128)}, f32[288,384]{1,0:T(8,128)}, f32[288,1152]{1,0:T(8,128)}, f32[288,3072]{1,0:T(8,128)},...) custom-call(bf16[8,4,7,16,128]{4,3,2,1,0:T(8,128)(2,1)} %get-tuple-element.90.refs_0_, ...), custom_call_target="tpu_custom_call" | custom-call | tf_op jit(solution)/shard_map/pallas_call | solution.py:1961
  (4 shorter events, 0.0 us)

commit v2 on v1

--- a/solution.py
+++ b/solution.py
@@ -437,7 +437,7 @@
     for at in range(last + 2):
         if at < last:
             gathers[at][0].to_pairs()
-        if at == last - 1:
+        if at == 0:
             start_background()
         if 1 <= at <= last:
             gathers[at - 1][0].to_sibling()
@@ -1600,8 +1600,10 @@
 
     sequences = units // KVH
     groups = wide // keys
-    for sequence in range(sequences):
-        span = slice(sequence * keys, (sequence + 1) * keys)
+    begin = pumped[0]
+
+    def query_rows(sequence):
+        span = pl.ds(pl.multiple_of(sequence * keys, LANES), keys)
         for pair in range(H // 2):
             heads = []
             for head in (2 * pair, 2 * pair + 1):
@@ -1611,12 +1613,15 @@
             query_all[fsdp, span, pair * 2 * HD : (pair + 1) * 2 * HD] = (
                 jnp.concatenate(heads, axis=0).astype(jnp.bfloat16).T
             )
-        pump_next(3)
+        tiles(3, lambda more: pump(begin + 3 * sequence + more))
+
+    tiles(sequences, query_rows)
+    pumped[0] += 3 * sequences
     query_gather.start(query_all.at[fsdp])
     combine(steps.levels)
     kv_width = KVH * HD
-    for sequence in range(sequences):
-        span = slice(sequence * keys, (sequence + 1) * keys)
+    def pair_rows(sequence):
+        span = pl.ds(pl.multiple_of(sequence * keys, LANES), keys)
         for pair in range(KVH // 2):
             turned_keys, turned_values = [], []
             for unit in (sequence * KVH + 2 * pair, sequence * KVH + 2 * pair + 1):
@@ -1627,6 +1632,7 @@
                 pair_all[fsdp, span, start + pair * 2 * HD : start + (pair + 1) * 2 * HD] = (
                     jnp.concatenate(parts, axis=0).astype(jnp.bfloat16).T
                 )
+    tiles(sequences, pair_rows)
     pair_gather.start(pair_all.at[fsdp])
     pump_next(2)
     query_gather.forward()

time: 350 us -> 348 us (level)
  no operation moved by 1% of the time
where the time goes in v2:
time: 348 us; the launch traced here: 347 us
  Pallas kernels  336 us (97%)
  local copies, waits for them, and re-layouts  9.05 us (3%)
    pallas_call x1, Pallas kernels, layer_back(): pl.pallas_call(functools.partial(back_kernel, [part.shape[0] for part in...  174 us
    pallas_call x1, Pallas kernels, attend(): pl.pallas_call(attend_kernel, out_shape=[jax.ShapeDtypeStruct((units, dee...  83.6 us
    pallas_call x1, Pallas kernels, feed_forward(): pl.pallas_call(ffn_kernel, out_shape=[jax.ShapeDtypeStruct((rows, width),...  69.6 us
    pallas_call x1, Pallas kernels, finish(): pl.pallas_call(functools.partial(finish_kernel, len(wides) // 2, len(down...  9.16 us

profile of v2, /device:TPU:0, one launch (start us, length us, event | category | flops | bytes accessed | tf_op | source)
XLA Modules:
  0.0 347.4 jit_solution(12071947715079031349)
XLA Ops:
  0.7 0.7 stack.9
  1.4 0.7 stack.10
  2.0 0.6 fusion.6.gain_ref
  2.7 0.8 multiply_sine_fusion
  3.4 1.9 copy.22
  5.3 1.9 copy.23
  7.3 83.6 %shard_map.194 = (bf16[12,128,384]{2,1,0:T(8,128)(2,1)}, bf16[1152,256]{1,0:T(8,128)(2,1)}, f32[1,1152]{1,0:T(1,128)}, f32[1,1152]{1,0:T(1,128)}, bf16[1152,1152...) custom-call(bf16[256,1152]{1,0:T(8,128)(2,1)} %bitcast.9, ...), custom_call_target="tpu_custom_call" | custom-call | tf_op jit(solution)/shard_map/pallas_call | solution.py:599
  90.9 69.6 %shard_map.195 = (f32[256,1152]{1,0:T(8,128)}, f32[256,1152]{1,0:T(8,128)}, bf16[256,1152]{1,0:T(8,128)(2,1)}, bf16[12,128,384]{2,1,0:T(8,128)(2,1)}, bf16[4,112...) custom-call(bf16[256,1152]{1,0:T(8,128)(2,1)} %bitcast.10, ...), custom_call_target="tpu_custom_call" | custom-call | tf_op jit(solution)/shard_map/pallas_call | solution.py:1228
  160.5 173.7 %shard_map.196 = (f32[256,1152]{1,0:T(8,128)}, bf16[256,1152]{1,0:T(8,128)(2,1)}, bf16[8,4,7,16,128]{4,3,2,1,0:T(8,128)(2,1)}, bf16[8,4,7,16,128]{4,3,2,1,0:T(8,...) custom-call(bf16[12,128,384]{2,1,0:T(8,128)(2,1)} %get-tuple-element, ...), custom_call_target="tpu_custom_call" | custom-call | tf_op jit(solution)/shard_map/pallas_call | solution.py:1813
  334.2 2.5 copy.26
  336.7 0.7 slice.12
  337.4 0.1 dynamic-slice_convert_fusion
  337.5 0.6 slice_reduce_fusion
  338.1 9.2 %shard_map.197 = (f32[288,1152]{1,0:T(8,128)}, f32[288,384]{1,0:T(8,128)}, f32[288,384]{1,0:T(8,128)}, f32[288,1152]{1,0:T(8,128)}, f32[288,3072]{1,0:T(8,128)},...) custom-call(bf16[8,4,7,16,128]{4,3,2,1,0:T(8,128)(2,1)} %get-tuple-element.90.refs_0_, ...), custom_call_target="tpu_custom_call" | custom-call | tf_op jit(solution)/shard_map/pallas_call | solution.py:1967
  (4 shorter events, 0.0 us)

commit v3 on v2

--- a/solution.py
+++ b/solution.py
@@ -257,8 +257,8 @@
 
 
 def attend_kernel(
-    x_ref, gain_ref, cos_ref, sin_ref, query_ref, key_ref, value_ref, out_ref, gate_ref, up_ref, g_ref,
-    q_ref, normed_t_ref, gain_attn_ref, gain_ffn_ref, full_query, full_key, full_value,
+    token_ref, upstream_ref, gain_ref, cos_ref, sin_ref, query_ref, key_ref, value_ref, out_ref, gate_ref,
+    up_ref, x_ref, q_ref, normed_t_ref, gain_attn_ref, gain_ffn_ref, full_query, full_key, full_value,
     low_ref, low_t_ref, mix_ref, log_ref, all_ref, full_out_ref, my_gate_ref, my_up_ref, all_g_ref,
     normed_ref, key_rows, gain_all, own_out, own_gate, own_up, own_g,
     top_ref, total_ref, chain_sends, chain_arrivals, peer_sends, peer_arrivals,
@@ -295,6 +295,9 @@
     ]
     for copy in own_copies:
         copy.start()
+    for sequence in range(sequences):
+        x_ref[sequence * keys : (sequence + 1) * keys] = token_ref[:, sequence, :]
+        own_g[sequence * keys : (sequence + 1) * keys] = upstream_ref[:, sequence, :]
     gain_all[fsdp] = gain_ref[...]
     pl.semaphore_wait(barrier, greeted)
 
@@ -400,8 +403,8 @@
         (out_ref, own_out, full_out_ref.at[own_rows]),
         (gate_ref.at[:, mine], own_gate, my_gate_ref.at[own_rows]),
         (up_ref.at[:, mine], own_up, my_up_ref.at[own_rows]),
-        (g_ref, own_g, all_g_ref.at[fsdp]),
     )
+    own_g_copy = pltpu.make_async_copy(own_g, all_g_ref.at[fsdp], local_sems.at[3])
     loads = [
         pltpu.make_async_copy(source, held, local_sems.at[at])
         for at, (source, held, _) in enumerate(own_parts)
@@ -431,7 +434,8 @@
         gathered.start(out_ref)
         for copy in slices:
             copy.start()
-        gathered_g.start(g_ref)
+        gathered_g.start(own_g)
+        own_g_copy.start()
 
     last = len(pieces)
     for at in range(last + 2):
@@ -563,6 +567,7 @@
     gathered_g.sent()
     for copy in slices:
         copy.wait()
+    own_g_copy.wait()
     for copy in background:
         copy.wait()
 
@@ -586,11 +591,11 @@
 VMEM = pl.BlockSpec(memory_space=pltpu.VMEM)
 
 
-def attend(x, gains, cosine, sine, w_query, w_key, w_value, w_out, w_gate, w_up, g_rows, sequences):
+def attend(tokens, upstream, gains, cosine, sine, w_query, w_key, w_value, w_out, w_gate, w_up):
     group, count = lax.axis_size("fsdp"), lax.axis_size("ctx")
-    rows, width = x.shape
+    keys, sequences, width = tokens.shape
     own, hidden = w_query.shape[0], w_gate.shape[1] // group
-    keys, units, deep = rows // sequences, sequences * KVH, 2 * HD
+    rows, units, deep = keys * sequences, sequences * KVH, 2 * HD
     wide = H // KVH * keys
     kv_width = KVH * HD
     dma = pltpu.SemaphoreType.DMA
@@ -599,6 +604,7 @@
     return pl.pallas_call(
         attend_kernel,
         out_shape=[
+            jax.ShapeDtypeStruct((rows, width), bf16),
             jax.ShapeDtypeStruct((units, deep, wide), bf16),
             jax.ShapeDtypeStruct((width, rows), bf16),
             jax.ShapeDtypeStruct((1, width), f32),
@@ -616,8 +622,8 @@
             jax.ShapeDtypeStruct((width, hidden), bf16),
             jax.ShapeDtypeStruct((group, rows, width), bf16),
         ],
-        in_specs=[VMEM] * 4 + [ANY] * 7,
-        out_specs=[VMEM] * 12 + [ANY] * 4,
+        in_specs=[VMEM] * 5 + [ANY] * 6,
+        out_specs=[VMEM] * 13 + [ANY] * 4,
         scratch_shapes=[
             pltpu.VMEM((rows, width), bf16),
             pltpu.VMEM((rows, kv_width), f32),
@@ -643,7 +649,7 @@
         compiler_params=pltpu.CompilerParams(
             collective_id=1, has_side_effects=True, vmem_limit_bytes=60 << 20
         ),
-    )(x, gains, cosine, sine, w_query, w_key, w_value, w_out, w_gate, w_up, g_rows)
+    )(tokens, upstream, gains, cosine, sine, w_query, w_key, w_value, w_out, w_gate, w_up)
 
 
 class Ring:
@@ -1870,8 +1876,8 @@
     def take(number):
         return [next(taken) for _ in range(number)]
 
-    wides, down_refs, smalls, (rows_ref,) = take(2 * halves), take(downs), take(4), take(1)
-    outs, (tokens_ref,) = take(7), take(1)
+    wides, down_refs, smalls, (rows_ref, layer_rows) = take(2 * halves), take(downs), take(4), take(2)
+    outs, (tokens_ref, layer_ref) = take(7), take(2)
     wide_held, down_held, small_held = take(2 * halves), take(downs), take(4)
     made, (load_sems, store_sems) = take(7), take(2)
     sources = [*wides, *down_refs, *smalls]
@@ -1950,12 +1956,14 @@
     store(2)
     keys = tokens_ref.shape[0]
     for sequence in range(tokens_ref.shape[1]):
-        tokens_ref[:, sequence, :] = rows_ref[sequence * keys : (sequence + 1) * keys]
+        block = slice(sequence * keys, (sequence + 1) * keys)
+        tokens_ref[:, sequence, :] = rows_ref[block]
+        layer_ref[:, sequence, :] = layer_rows[block]
     for copy in stores:
         copy.wait()
 
 
-def finish(wides, downs, smalls, token_rows, own, kv_width, hidden, sequences):
+def finish(wides, downs, smalls, token_rows, layer_rows, own, kv_width, hidden, sequences):
     rows, width = token_rows.shape
     f32 = jnp.float32
     outs = [
@@ -1966,14 +1974,18 @@
     dma = pltpu.SemaphoreType.DMA
     return pl.pallas_call(
         functools.partial(finish_kernel, len(wides) // 2, len(downs)),
-        out_shape=outs + [jax.ShapeDtypeStruct((rows // sequences, sequences, width), f32)],
-        in_specs=[ANY] * len(sources) + [VMEM],
-        out_specs=[ANY] * len(outs) + [VMEM],
+        out_shape=outs
+        + [
+            jax.ShapeDtypeStruct((rows // sequences, sequences, width), kind)
+            for kind in (f32, layer_rows.dtype)
+        ],
+        in_specs=[ANY] * len(sources) + [VMEM] * 2,
+        out_specs=[ANY] * len(outs) + [VMEM] * 2,
         scratch_shapes=[pltpu.VMEM(array.shape, array.dtype) for array in sources]
         + [pltpu.VMEM(out.shape, f32) for out in outs]
         + [dma((len(sources),)), dma((5 + 2 * wides[0].shape[1],))],
         compiler_params=pltpu.CompilerParams(vmem_limit_bytes=60 << 20),
-    )(*sources, token_rows)
+    )(*sources, token_rows, layer_rows)
 
 
 def on_device(
@@ -1986,8 +1998,6 @@
     freqs = ROTARY_BASE ** (-2.0 * jnp.arange(HD // 2, dtype=jnp.float32) / HD)
     angles = freqs[:, None] * positions.astype(jnp.float32)[None, :]
     cosine, sine = jnp.cos(angles), jnp.sin(angles)
-    x_rows = jnp.swapaxes(tokens, 0, 1).reshape(rows_count, width)
-    g_rows = jnp.swapaxes(cotangent, 0, 1).reshape(rows_count, width)
     own = gain_attn.shape[0]
     units = seq_count * KVH
     wide = H // KVH * block_len
@@ -1995,10 +2005,10 @@
         jnp.stack([gain_attn, gain_ffn]).astype(jnp.float32), ((0, 6), (0, spread(own, LANES) - own))
     )
     (
-        q_wide, normed_t, full_gain_attn, full_gain_ffn, full_query, full_key, full_value, attn_low, low_t, mix_unit, log_total,
+        x_rows, q_wide, normed_t, full_gain_attn, full_gain_ffn, full_query, full_key, full_value, attn_low, low_t, mix_unit, log_total,
         all_pairs, full_out, my_gate, my_up, all_g,
     ) = attend(
-        x_rows, own_gains, cosine, sine, w_query, w_key, w_value, w_out, w_gate, w_up, g_rows, seq_count
+        tokens, cotangent, own_gains, cosine, sine, w_query, w_key, w_value, w_out, w_gate, w_up
     )
     layer_base, grad_resid, grad_branch, g_wide, gate_part, up_part, layer_parts, *downs = (
         feed_forward(
@@ -2017,11 +2027,12 @@
     gain_grads = smalls[2][filled:].reshape(-1, LANES)[: 2 * (width // LANES)].reshape(2, width)
     gain_grads = lax.dynamic_slice_in_dim(gain_grads, lax.axis_index("fsdp") * own, own, 1)
     gain_grads = gain_grads.astype(jnp.float32)
-    *grads, tokens_grad = finish(
-        wides, sums[: len(downs)], smalls, grad_tokens, own, kv_width, w_down.shape[0], seq_count
+    *grads, tokens_grad, layer_result = finish(
+        wides, sums[: len(downs)], smalls, grad_tokens, layer_out, own, kv_width, w_down.shape[0],
+        seq_count,
     )
     return (
-        jnp.swapaxes(layer_out.reshape(seq_count, block_len, width), 0, 1),
+        layer_result,
         tokens_grad,
         *grads,
         gain_grads[0],

time: 348 us -> 343 us (0.986)
  local copies, waits for them, and re-layouts: 9.05 us -> 2.69 us
    transpose x2 -> x0, local copies, waits for them, and re-layouts: 3.88 us -> none  [the longest x1 1.94 us: on_device(): x_rows = jnp.swapaxes(tokens, 0, 1).reshape(rows_count, width)]
where the time goes in v3:
time: 343 us
  Pallas kernels  338 us (99%)
    pallas_call x1, Pallas kernels, layer_back(): pl.pallas_call(functools.partial(back_kernel, [part.shape[0] for part in...  174 us
    pallas_call x1, Pallas kernels, attend(): pl.pallas_call(attend_kernel, out_shape=[jax.ShapeDtypeStruct((rows, widt...  85.4 us
    pallas_call x1, Pallas kernels, feed_forward(): pl.pallas_call(ffn_kernel, out_shape=[jax.ShapeDtypeStruct((rows, width),...  68.6 us
    pallas_call x1, Pallas kernels, finish(): pl.pallas_call(functools.partial(finish_kernel, len(wides) // 2, len(down...  9.5 us

profile of v3, /device:TPU:0, one launch (start us, length us, event | category | flops | bytes accessed | tf_op | source)
XLA Modules:
  0.0 342.6 jit_solution(6434152270955001553)
XLA Ops:
  0.7 0.7 stack.9
  1.4 0.7 stack.10
  2.0 0.6 fusion.6.gain_ref
  2.7 0.8 multiply_sine_fusion
  3.4 85.4 %shard_map.194 = (bf16[256,1152]{1,0:T(8,128)(2,1)}, bf16[12,128,384]{2,1,0:T(8,128)(2,1)}, bf16[1152,256]{1,0:T(8,128)(2,1)}, f32[1,1152]{1,0:T(1,128)}, f32[1,...) custom-call(bf16[128,2,1152]{2,1,0:T(2,128)(2,1)} %token_ref.1, ...), custom_call_target="tpu_custom_call" | custom-call | tf_op jit(solution)/shard_map/pallas_call | solution.py:604
  88.8 68.6 %shard_map.195 = (f32[256,1152]{1,0:T(8,128)}, f32[256,1152]{1,0:T(8,128)}, bf16[256,1152]{1,0:T(8,128)(2,1)}, bf16[12,128,384]{2,1,0:T(8,128)(2,1)}, bf16[4,112...) custom-call(bf16[256,1152]{1,0:T(8,128)(2,1)} %get-tuple-element.64., ...), custom_call_target="tpu_custom_call" | custom-call | tf_op jit(solution)/shard_map/pallas_call | solution.py:1234
  157.5 174.0 %shard_map.196 = (f32[256,1152]{1,0:T(8,128)}, bf16[256,1152]{1,0:T(8,128)(2,1)}, bf16[8,4,7,16,128]{4,3,2,1,0:T(8,128)(2,1)}, bf16[8,4,7,16,128]{4,3,2,1,0:T(8,...) custom-call(bf16[12,128,384]{2,1,0:T(8,128)(2,1)} %get-tuple-element, ...), custom_call_target="tpu_custom_call" | custom-call | tf_op jit(solution)/shard_map/pallas_call | solution.py:1819
  331.5 0.7 slice.12
  332.2 0.1 dynamic-slice_convert_fusion
  332.3 0.6 slice_reduce_fusion
  332.9 9.5 %shard_map.197 = (f32[288,1152]{1,0:T(8,128)}, f32[288,384]{1,0:T(8,128)}, f32[288,384]{1,0:T(8,128)}, f32[288,1152]{1,0:T(8,128)}, f32[288,3072]{1,0:T(8,128)},...) custom-call(bf16[8,4,7,16,128]{4,3,2,1,0:T(8,128)(2,1)} %get-tuple-element., ...), custom_call_target="tpu_custom_call" | custom-call | tf_op jit(solution)/shard_map/pallas_call | solution.py:1975
  (4 shorter events, 0.0 us)

commit v4 on v3

--- a/solution.py
+++ b/solution.py
@@ -297,7 +297,6 @@
         copy.start()
     for sequence in range(sequences):
         x_ref[sequence * keys : (sequence + 1) * keys] = token_ref[:, sequence, :]
-        own_g[sequence * keys : (sequence + 1) * keys] = upstream_ref[:, sequence, :]
     gain_all[fsdp] = gain_ref[...]
     pl.semaphore_wait(barrier, greeted)
 
@@ -316,6 +315,8 @@
         gain_copy(step).start()
     for gather, source in gathers:
         gather.start(source)
+    for sequence in range(sequences):
+        own_g[sequence * keys : (sequence + 1) * keys] = upstream_ref[:, sequence, :]
     inputs = x_ref[...].astype(jnp.float32)
     scale = norm_scale(inputs)
     q_ref[:, HD:, :] = jnp.zeros((units, HD, wide), q_ref.dtype)
@@ -1755,9 +1756,9 @@
         tiles(rows // 32, close)
 
     def last_ticks(at, unused):
-        tiles(half, lambda turn: pump(jnp.minimum(begun + half * at + turn, total_pumps)))
         tick(rest_a, at)
         tick(rest_b, at)
+        tiles(half, lambda turn: pump(jnp.minimum(begun + half * at + turn, total_pumps)))
 
         @pl.when(at == rest_a.ticks * 3 // 4)
         def _():

time: 343 us -> 342 us (level)
  no operation moved by 1% of the time
where the time goes in v4:
time: 342 us
  Pallas kernels  337 us (99%)
    pallas_call x1, Pallas kernels, layer_back(): pl.pallas_call(functools.partial(back_kernel, [part.shape[0] for part in...  173 us
    pallas_call x1, Pallas kernels, attend(): pl.pallas_call(attend_kernel, out_shape=[jax.ShapeDtypeStruct((rows, widt...  84.1 us
    pallas_call x1, Pallas kernels, feed_forward(): pl.pallas_call(ffn_kernel, out_shape=[jax.ShapeDtypeStruct((rows, width),...  69.5 us
    pallas_call x1, Pallas kernels, finish(): pl.pallas_call(functools.partial(finish_kernel, len(wides) // 2, len(down...  9.5 us

profile of v4, /device:TPU:0, one launch (start us, length us, event | category | flops | bytes accessed | tf_op | source)
XLA Modules:
  0.0 341.6 jit_solution(13939507172670878733)
XLA Ops:
  0.7 0.7 stack.9
  1.4 0.7 stack.10
  2.0 0.6 fusion.6.gain_ref
  2.7 0.8 multiply_sine_fusion
  3.4 84.1 %shard_map.194 = (bf16[256,1152]{1,0:T(8,128)(2,1)}, bf16[12,128,384]{2,1,0:T(8,128)(2,1)}, bf16[1152,256]{1,0:T(8,128)(2,1)}, f32[1,1152]{1,0:T(1,128)}, f32[1,...) custom-call(bf16[128,2,1152]{2,1,0:T(2,128)(2,1)} %token_ref.1, ...), custom_call_target="tpu_custom_call" | custom-call | tf_op jit(solution)/shard_map/pallas_call | solution.py:605
  87.5 69.5 %shard_map.195 = (f32[256,1152]{1,0:T(8,128)}, f32[256,1152]{1,0:T(8,128)}, bf16[256,1152]{1,0:T(8,128)(2,1)}, bf16[12,128,384]{2,1,0:T(8,128)(2,1)}, bf16[4,112...) custom-call(bf16[256,1152]{1,0:T(8,128)(2,1)} %get-tuple-element.64., ...), custom_call_target="tpu_custom_call" | custom-call | tf_op jit(solution)/shard_map/pallas_call | solution.py:1235
  157.0 173.4 %shard_map.196 = (f32[256,1152]{1,0:T(8,128)}, bf16[256,1152]{1,0:T(8,128)(2,1)}, bf16[8,4,7,16,128]{4,3,2,1,0:T(8,128)(2,1)}, bf16[8,4,7,16,128]{4,3,2,1,0:T(8,...) custom-call(bf16[12,128,384]{2,1,0:T(8,128)(2,1)} %get-tuple-element, ...), custom_call_target="tpu_custom_call" | custom-call | tf_op jit(solution)/shard_map/pallas_call | solution.py:1820
  330.5 0.7 slice.12
  331.2 0.1 dynamic-slice_convert_fusion
  331.3 0.6 slice_reduce_fusion
  331.9 9.5 %shard_map.197 = (f32[288,1152]{1,0:T(8,128)}, f32[288,384]{1,0:T(8,128)}, f32[288,384]{1,0:T(8,128)}, f32[288,1152]{1,0:T(8,128)}, f32[288,3072]{1,0:T(8,128)},...) custom-call(bf16[8,4,7,16,128]{4,3,2,1,0:T(8,128)(2,1)} %get-tuple-element., ...), custom_call_target="tpu_custom_call" | custom-call | tf_op jit(solution)/shard_map/pallas_call | solution.py:1976
  (4 shorter events, 0.0 us)

commit v5 on v4

--- a/solution.py
+++ b/solution.py
@@ -2003,7 +2003,7 @@
     units = seq_count * KVH
     wide = H // KVH * block_len
     own_gains = jnp.pad(
-        jnp.stack([gain_attn, gain_ffn]).astype(jnp.float32), ((0, 6), (0, spread(own, LANES) - own))
+        jnp.concatenate([gain_attn, gain_ffn]).reshape(2, own).astype(jnp.float32), ((0, 6), (0, spread(own, LANES) - own))
     )
     (
         x_rows, q_wide, normed_t, full_gain_attn, full_gain_ffn, full_query, full_key, full_value, attn_low, low_t, mix_unit, log_total,

time: 342 us -> 342 us (level)
  no operation moved by 1% of the time
where the time goes in v5:
time: 342 us; the launch traced here: 341 us
  Pallas kernels  337 us (99%)
    pallas_call x1, Pallas kernels, layer_back(): pl.pallas_call(functools.partial(back_kernel, [part.shape[0] for part in...  174 us
    pallas_call x1, Pallas kernels, attend(): pl.pallas_call(attend_kernel, out_shape=[jax.ShapeDtypeStruct((rows, widt...  84.1 us
    pallas_call x1, Pallas kernels, feed_forward(): pl.pallas_call(ffn_kernel, out_shape=[jax.ShapeDtypeStruct((rows, width),...  69.4 us
    pallas_call x1, Pallas kernels, finish(): pl.pallas_call(functools.partial(finish_kernel, len(wides) // 2, len(down...  9.5 us

profile of v5, /device:TPU:0, one launch (start us, length us, event | category | flops | bytes accessed | tf_op | source)
XLA Modules:
  0.0 341.0 jit_solution(12170765014776489319)
XLA Ops:
  0.7 0.8 pad_maximum_fusion
  1.4 0.1 convert_element_type.16
  1.5 0.6 pad_convert_fusion.gain_ref
  2.1 0.8 multiply_sine_fusion
  2.9 84.1 %shard_map.194 = (bf16[256,1152]{1,0:T(8,128)(2,1)}, bf16[12,128,384]{2,1,0:T(8,128)(2,1)}, bf16[1152,256]{1,0:T(8,128)(2,1)}, f32[1,1152]{1,0:T(1,128)}, f32[1,...) custom-call(bf16[128,2,1152]{2,1,0:T(2,128)(2,1)} %token_ref.1, ...), custom_call_target="tpu_custom_call" | custom-call | tf_op jit(solution)/shard_map/pallas_call | solution.py:605
  87.0 69.4 %shard_map.195 = (f32[256,1152]{1,0:T(8,128)}, f32[256,1152]{1,0:T(8,128)}, bf16[256,1152]{1,0:T(8,128)(2,1)}, bf16[12,128,384]{2,1,0:T(8,128)(2,1)}, bf16[4,112...) custom-call(bf16[256,1152]{1,0:T(8,128)(2,1)} %get-tuple-element.64., ...), custom_call_target="tpu_custom_call" | custom-call | tf_op jit(solution)/shard_map/pallas_call | solution.py:1235
  156.4 173.6 %shard_map.196 = (f32[256,1152]{1,0:T(8,128)}, bf16[256,1152]{1,0:T(8,128)(2,1)}, bf16[8,4,7,16,128]{4,3,2,1,0:T(8,128)(2,1)}, bf16[8,4,7,16,128]{4,3,2,1,0:T(8,...) custom-call(bf16[12,128,384]{2,1,0:T(8,128)(2,1)} %get-tuple-element, ...), custom_call_target="tpu_custom_call" | custom-call | tf_op jit(solution)/shard_map/pallas_call | solution.py:1820
  329.9 0.7 slice.12
  330.7 0.1 dynamic-slice_convert_fusion
  330.7 0.6 slice_reduce_fusion
  331.3 9.5 %shard_map.197 = (f32[288,1152]{1,0:T(8,128)}, f32[288,384]{1,0:T(8,128)}, f32[288,384]{1,0:T(8,128)}, f32[288,1152]{1,0:T(8,128)}, f32[288,3072]{1,0:T(8,128)},...) custom-call(bf16[8,4,7,16,128]{4,3,2,1,0:T(8,128)(2,1)} %get-tuple-element., ...), custom_call_target="tpu_custom_call" | custom-call | tf_op jit(solution)/shard_map/pallas_call | solution.py:1976
  (4 shorter events, 0.0 us)
